TPU v7x, 256 devices: a whole 4x4x8 slice. The times are simulated.
256 devices in a mesh: queue: 16 (over z, y_hi), space: 16 (over y_lo, x, core).
Axes of the slice: x: 4, y: 4 (y_hi: 2, y_lo: 2; y = y_hi * 2 + y_lo), z: 8, core: 2. Of those that a mesh axis runs over, the one named last changes fastest.
Arguments:
- latents: float32 [16, 128, 8, 64], P('queue', 'space'), may hold values from -6 to 6
- fresh_noise: float32 [1, 128, 64], P(None, 'space'), may hold values from -6 to 6
- levels: int32 [16, 8], replicated, may hold values from 0 to 999, as said below
- patch_weight: bfloat16 [64, 3072], replicated, may hold values from -0.75 to 0.75
- time_weight: bfloat16 [3072, 512], P(None, 'space'), may hold values from -0.109375 to 0.109375
- adaln_weight: bfloat16 [512, 6, 3072], P('space'), may hold values from -0.5 to 0.5
- qkv_weight: bfloat16 [3072, 3, 3072], P(None, None, 'space'), may hold values from -0.109375 to 0.109375
- out_weight: bfloat16 [3072, 3072], P('space'), may hold values from -0.75 to 0.75
- up_weight: bfloat16 [3072, 6144], P(None, 'space'), may hold values from -0.109375 to 0.109375
- down_weight: bfloat16 [6144, 3072], P('space'), may hold values from -0.21875 to 0.21875
- proj_weight: bfloat16 [3072, 64], replicated, may hold values from -0.109375 to 0.109375
Outputs:
- latents_out: float32 [16, 128, 8, 64], P('queue', 'space')
- predictions: float32 [1, 16, 128, 8, 64], P(None, 'queue', 'space')
Inputs may be any that keep to these rules, and one draw needn't show every extreme that they name: levels fall strictly along the queue order q * 8 + f; the first is 999 and the last is 0.
All inputs are finite; a program needn't handle non-finite values.
Results may differ from a plain program's by a relative error of at most 0.03.
Values may be sent and summed in bfloat16 or wider, within the bound.
A program may use at most 128 MiB of HBM per device.

v0:
```python
import math

import jax
import jax.numpy as jnp
from jax import lax
from jax.sharding import PartitionSpec as P

HD = 64
NT = 1000


def shifted(block, axis, distance):
    devices = range(lax.axis_size(axis))
    route = [(i - distance, i) for i in devices if i - distance in devices]
    return lax.ppermute(block, axis, route)


def noise_level(times):
    angle = (times / NT + 0.008) / 1.008 * (math.pi / 2)
    cosine = jnp.cos(angle)
    return 0.05 + 0.94 * cosine * cosine


def step_scales(levels):
    flat = levels.reshape(-1)
    later = jnp.concatenate([flat[1:], jnp.full((1,), -1, jnp.int32)])
    now = noise_level(flat.astype(jnp.float32))
    after = jnp.where(later < 0, jnp.float32(1.0), noise_level(later.astype(jnp.float32)))
    keep = jnp.sqrt(after / now)
    mix = jnp.sqrt(1.0 - after) - jnp.sqrt(after * (1.0 - now) / now)
    return (keep.reshape(levels.shape), mix.reshape(levels.shape))


def time_features(times, width):
    half = width // 2
    freqs = jnp.exp(-math.log(10000.0) * jnp.arange(half, dtype=jnp.float32) / half)
    angle = times.astype(jnp.float32)[:, None] * freqs[None, :]
    return jnp.concatenate([jnp.cos(angle), jnp.sin(angle)], -1)


def layer_norm(values, epsilon):
    centre = values - jnp.mean(values, -1, keepdims=True)
    spread = jnp.mean(centre * centre, -1, keepdims=True)
    return centre * lax.rsqrt(spread + epsilon)


def attention(projected, heads):
    total_rows = projected.shape[0]
    split = projected.reshape(total_rows, 3, heads, HD)
    queries = layer_norm(split[:, 0], 1e-06).astype(jnp.bfloat16)
    keys = layer_norm(split[:, 1], 1e-06).astype(jnp.bfloat16)
    values = split[:, 2].astype(jnp.bfloat16)
    scores = jnp.einsum("qhd,khd->hqk", queries, keys, preferred_element_type=jnp.float32) * HD ** (
        -0.5
    )
    weights = jnp.exp(scores)
    probs = (weights / jnp.sum(weights, -1, keepdims=True)).astype(jnp.bfloat16)
    mixed = jnp.einsum("hqk,khd->qhd", probs, values, preferred_element_type=jnp.float32)
    return mixed.astype(jnp.bfloat16).reshape(total_rows, heads * HD)


def modulate(hidden, shift_vec, scale_vec):
    return (layer_norm(hidden, 1e-05) * (1.0 + scale_vec) + shift_vec).astype(jnp.bfloat16)


def queue_turn(state, noise_frame, modulation, keep, mix, queue_here, weights):
    patch_weight, qkv_weight, out_weight, up_weight, down_weight, proj_weight = weights
    positions, frames, channels = state.shape
    width = patch_weight.shape[1]
    rows_dev = positions * frames
    wide_qkv = qkv_weight.reshape(width, -1)
    heads_dev = qkv_weight.shape[2] // HD
    count_rows = state.shape[0]
    flat = state.astype(jnp.bfloat16).reshape(count_rows * frames, channels)
    residual = jnp.dot(flat, patch_weight, preferred_element_type=jnp.float32).reshape(
        count_rows, frames, width
    )
    normed = modulate(residual, modulation[:, 0], modulation[:, 1])
    piece = lax.all_gather(normed, "space", axis=0, tiled=True)
    count_rows = piece.shape[0]
    product = jnp.dot(
        piece.reshape(count_rows * frames, width), wide_qkv, preferred_element_type=jnp.float32
    )
    projected = product.reshape(count_rows, frames, -1)
    total_rows = projected.shape[0] * frames
    mixed = attention(projected.reshape(total_rows, -1), heads_dev)
    attended = lax.psum_scatter(
        jnp.dot(mixed, out_weight, preferred_element_type=jnp.float32).astype(jnp.bfloat16),
        "space",
        scatter_dimension=0,
        tiled=True,
    ).astype(jnp.float32)
    residual = residual + modulation[:, 2] * attended.reshape(positions, frames, width)
    piece = lax.all_gather(
        modulate(residual, modulation[:, 3], modulation[:, 4]), "space", axis=0, tiled=True
    )
    count_rows = piece.shape[0]
    product = jnp.dot(
        piece.reshape(count_rows * frames, width), up_weight, preferred_element_type=jnp.float32
    )
    expanded = (
        jax.nn.gelu(product, approximate=True).astype(jnp.bfloat16).reshape(count_rows, frames, -1)
    )
    flat_hidden = expanded.reshape(total_rows, -1)
    fed = lax.psum_scatter(
        jnp.dot(flat_hidden, down_weight, preferred_element_type=jnp.float32).astype(jnp.bfloat16),
        "space",
        scatter_dimension=0,
        tiled=True,
    ).astype(jnp.float32)
    residual = residual + modulation[:, 5] * fed.reshape(positions, frames, width)
    final = layer_norm(residual, 1e-05).astype(jnp.bfloat16).reshape(rows_dev, width)
    predicted = jnp.dot(final, proj_weight, preferred_element_type=jnp.float32).reshape(
        positions, frames, channels
    )
    moved = keep[None, :, None] * state + mix[None, :, None] * predicted
    carried = shifted(moved[:, frames - 1], "queue", 1)
    entering = jnp.where(queue_here == 0, noise_frame, carried)
    return (jnp.concatenate([entering[:, None], moved[:, : frames - 1]], 1), predicted)


def body(
    latents,
    fresh_noise,
    levels,
    patch_weight,
    time_weight,
    adaln_weight,
    qkv_weight,
    out_weight,
    up_weight,
    down_weight,
    proj_weight,
):
    queue_here = lax.axis_index("queue")
    width = patch_weight.shape[1]
    keep_all, mix_all = step_scales(levels)
    keep = lax.dynamic_index_in_dim(keep_all, queue_here, 0, keepdims=False)
    mix = lax.dynamic_index_in_dim(mix_all, queue_here, 0, keepdims=False)
    level_here = lax.dynamic_index_in_dim(levels, queue_here, 0, keepdims=False)
    features = time_features(level_here, width).astype(jnp.bfloat16)
    timing = jax.nn.silu(jnp.dot(features, time_weight, preferred_element_type=jnp.float32)).astype(
        jnp.bfloat16
    )
    partial_terms = jnp.einsum(
        "fe,ekd->fkd", timing, adaln_weight, preferred_element_type=jnp.float32
    )
    modulation = lax.psum(partial_terms, "space")
    weights = (patch_weight, qkv_weight, out_weight, up_weight, down_weight, proj_weight)
    state = latents[0]
    state, predicted = queue_turn(state, fresh_noise[0], modulation, keep, mix, queue_here, weights)
    collected = [predicted]
    return (state[None], jnp.stack(collected)[:, None])


def solution(mesh):
    in_specs = (
        P("queue", "space", None, None),
        P(None, "space", None),
        P(),
        P(),
        P(None, "space"),
        P("space", None, None),
        P(None, None, "space"),
        P("space", None),
        P(None, "space"),
        P("space", None),
        P(),
    )
    out_specs = (P("queue", "space", None, None), P(None, "queue", "space", None, None))
    return jax.shard_map(body, mesh=mesh, in_specs=in_specs, out_specs=out_specs, check_vma=False)
```

profile of v0, /device:TPU:1, one launch (start us, length us, event | category | flops | bytes accessed | tf_op | source)
XLA Modules:
  0.0 426.3 jit_solution(11909300190902213185)
XLA Ops:
  7.2 1.0 convert_reduce_fusion
  8.3 0.9 fusion.39
  9.2 2.8 fusion.55
  12.0 1.3 fusion.69
  13.4 0.9 copy-done.3
  14.5 121.8 %all-reduce.2.cloned.1.call-done = f32[8,6,3072]{2,0,1:T(8,128)} async-done(((f32[8,6,3072]{2,0,1:T(8,128)}), f32[8,6,3072]{2,0,1:T(8,128)}) %all-reduce.2.cloned.1.call-update) | async-done | bytes 589840 | tf_op jit(solution)/shard_map/psum | solution.py:148
  136.3 1.9 slice_bitcast_fusion.1
  138.1 2.1 add_convert_fusion.1
  140.3 49.3 %all-gather.3.cloned.1.call-done = bf16[128,8,3072]{2,1,0:T(8,128)(2,1)} async-done(((bf16[8,8,3072]{2,1,0:T(8,128)(2,1)}), bf16[128,8,3072]{2,1,0:T(8,128)(2,1)}) %all-gather.3.cloned.1.call-update) | async-done | bytes 6291472 | tf_op jit(solution)/shard_map/all_gather | solution.py:79
  189.6 6.0 %fusion.1 = f32[1024,3,3,64]{0,3,2,1:T(8,128)S(1)} fusion(bf16[3,3,64,3072]{3,2,1,0:T(8,128)(2,1)S(1)} %bitcast.126, bf16[128,8,3072]{2,1,0:T(8,128)(2,1)} %all-gather.3.cloned.1.call-done), kind=kOutput, calls=%fused_computation.3 | convolution fusion | flops 3623878656 | bytes 12189696 | tf_op jit(solution)/shard_map/dot_general | solution.py:81
  196.1 2.1 fusion
  198.2 2.3 fusion.16
  200.5 4.5 %convolution_convert_fusion = bf16[1024,3072]{1,0:T(8,128)(2,1)} fusion(bf16[1024,192]{0,1:T(8,128)(2,1)S(1)} %bitcast.127, bf16[192,3072]{1,0:T(8,128)(2,1)S(1)} %copy-done.6), kind=kOutput, calls=%fused_computation.8 | convolution fusion | flops 1211105280 | bytes 7864320 | tf_op jit(solution)/shard_map/dot_general | solution.py:88
  205.1 70.2 %reduce-scatter.3.cloned.1.call-done = bf16[64,3072]{1,0:T(8,128)(2,1)} async-done(((bf16[1024,3072]{1,0:T(8,128)(2,1)}), bf16[64,3072]{1,0:T(8,128)(2,1)}) %reduce-scatter.3.cloned.1.call-update) | async-done | bytes 393232 | tf_op jit(solution)/shard_map/reduce_scatter | solution.py:87
  275.3 1.5 fusion.67
  277.0 0.7 copy-done.1
  277.7 1.0 add_convert_fusion
  278.9 47.4 %all-gather.5.cloned.1.call-done = bf16[128,8,3072]{2,1,0:T(8,128)(2,1)} async-done(((bf16[8,8,3072]{2,1,0:T(8,128)(2,1)}), bf16[128,8,3072]{2,1,0:T(8,128)(2,1)}) %all-gather.5.cloned.1.call-update) | async-done | bytes 6291472 | tf_op jit(solution)/shard_map/all_gather | solution.py:94
  326.3 12.0 %convolution_convert_fusion.1 = bf16[1024,3072]{1,0:T(8,128)(2,1)} fusion(bf16[384,3072]{1,0:T(8,128)(2,1)} %param.20, bf16[3072,384]{1,0:T(8,128)(2,1)} %param.19, bf16[128,8,3072]{2,1,0:T(8,128)(2,1)} %all-gather.5.cloned.1.call-done), kind=kOutput, calls=%fused_computation.9 | convolution fusion | flops 4838522880 | bytes 17301504 | tf_op jit(solution)/shard_map/dot_general | solution.py:106
  338.3 0.7 copy-done.12
  339.7 0.6 multiply_cosine_fusion.1
  340.4 0.7 reshape.162
  341.1 1.3 broadcast_compare_fusion
  342.4 1.3 lt.20
  343.7 0.7 fusion.47
  344.5 64.1 %reduce-scatter.5.cloned.1.call-done = bf16[64,3072]{1,0:T(8,128)(2,1)} async-done(((bf16[1024,3072]{1,0:T(8,128)(2,1)}), bf16[64,3072]{1,0:T(8,128)(2,1)}) %reduce-scatter.5.cloned.1.call-update) | async-done | bytes 393232 | tf_op jit(solution)/shard_map/reduce_scatter | solution.py:105
  408.6 1.6 fusion.36
  410.2 1.5 multiply_reduce_fusion
  411.7 1.0 fusion.45
  413.3 4.3 %collective-permute-start = (f32[8,64]{1,0:T(8,128)S(1)}, f32[8,64]{1,0:T(8,128)S(1)}, u32[]{:S(2)}, u32[]{:S(2)}) collective-permute-start(f32[8,64]{1,0:T(8,128)S(1)} %bitcast.131), channel_id=1, source_target_pairs={{0,16},{16,32},{32,48},{48,64},{64,80},{80,96},{96,112},{112,128},... | collective-permute-start | bytes 6152 | tf_op jit(solution)/shard_map/ppermute | solution.py:15
  417.6 0.7 collective-permute-done
  418.4 1.4 maximum_bitcast_fusion
  (57 shorter events, 2.9 us)
Async XLA Ops:
  7.2 182.5 %copy-start = (bf16[3072,3,192]{0,2,1:T(8,128)(2,1)S(1)}, bf16[3072,3,192]{0,2,1:T(8,128)(2,1)}, u32[]{:S(2)}) copy-start(bf16[3072,3,192]{0,2,1:T(8,128)(2,1)} %param.17) | copy-start | bytes 10616836
  7.2 129.1 %all-reduce.2.cloned.1.call-start = ((), (), s32[]{:S(2)}) async-start(), calls=%async_computation.2 | async-start | bytes 1179648 | tf_op jit(solution)/shard_map/psum | solution.py:148
  11.9 177.7 %all-gather.3.cloned.1.call-start = ((), (), s32[]{:S(2)}) async-start(), calls=%async_computation.3 | async-start | bytes 6684672 | tf_op jit(solution)/shard_map/all_gather | solution.py:79
  13.3 0.9 copy-start.3
  140.2 135.0 %reduce-scatter.3.cloned.1.call-start = ((), (), s32[]{:S(2)}) async-start(), calls=%async_computation.4 | async-start | bytes 6684672 | tf_op jit(solution)/shard_map/reduce_scatter | solution.py:87
  198.2 2.3 copy-start.6
  205.0 121.3 %all-gather.5.cloned.1.call-start = ((), (), s32[]{:S(2)}) async-start(), calls=%async_computation.5 | async-start | bytes 6684672 | tf_op jit(solution)/shard_map/all_gather | solution.py:94
  275.3 2.4 copy-start.8
  275.3 2.4 copy-start.9
  276.8 0.9 copy-start.1
  278.7 129.9 %reduce-scatter.5.cloned.1.call-start = ((), (), s32[]{:S(2)}) async-start(), calls=%async_computation.6 | async-start | bytes 6684672 | tf_op jit(solution)/shard_map/reduce_scatter | solution.py:105
  338.3 0.7 copy-start.12
  339.2 0.5 copy-start.14
  344.4 73.9 %copy-start.13 = (f32[1,8,64]{2,1,0:T(8,128)S(1)}, f32[1,8,64]{2,1,0:T(8,128)}, u32[]{:S(2)}) copy-start(f32[1,8,64]{2,1,0:T(8,128)} %param.12) | copy-start | bytes 6148
  408.6 3.1 copy-start.2
  408.6 3.1 copy-start.4
  408.6 3.1 copy-start.5
  408.6 3.1 copy-start.7
  408.6 3.1 copy-start.11
  412.7 0.6 copy-start.10
  413.3 5.1 %collective-permute-start = (f32[8,64]{1,0:T(8,128)S(1)}, f32[8,64]{1,0:T(8,128)S(1)}, u32[]{:S(2)}, u32[]{:S(2)}) collective-permute-start(f32[8,64]{1,0:T(8,128)S(1)} %bitcast.131), channel_id=1, source_target_pairs={{0,16},{16,32},{32,48},{48,64},{64,80},{80,96},{96,112},{112,128},... | collective-permute-start | bytes 6152 | tf_op jit(solution)/shard_map/ppermute | solution.py:15
Sparse Core Ops, SparseCore 0:
  12.1 124.1 all-reduce.1
  140.4 49.2 all-gather.2
  205.2 70.0 reduce-scatter.2
  278.8 47.4 all-gather.4
  338.5 70.1 reduce-scatter.4
where the time goes:
time: 432 us; the launch traced here: 426 us
  waiting for transfers between devices  354 us (82%)
  matrix products  31.9 us (7%)
  other arithmetic  16.4 us (4%)
  between operations  14 us (3%)
  local copies, waits for them, and re-layouts  5.67 us (1%)
  starting transfers between devices  4.72 us (1%)
    psum x1, waiting for transfers between devices, body(): modulation = lax.psum(partial_terms, 'space')  122 us
    reduce_scatter x1, waiting for transfers between devices, queue_turn(): lax.psum_scatter(jnp.dot(mixed, out_weight, preferred_element_type=jnp.fl...  70.2 us
    reduce_scatter x1, waiting for transfers between devices, queue_turn(): lax.psum_scatter(jnp.dot(flat_hidden, down_weight, preferred_element_type...  64.1 us
    all_gather x1, waiting for transfers between devices, queue_turn(): piece = lax.all_gather(normed, 'space', axis=0, tiled=True)  49.3 us
    all_gather x1, waiting for transfers between devices, queue_turn(): lax.all_gather(modulate(residual, modulation[:, 3], modulation[:, 4]), 's...  47.4 us
    dot_general x1, matrix products, queue_turn(): jnp.dot(flat_hidden, down_weight, preferred_element_type=jnp.float32)  12 us
  transfers between devices with their start and end apart: 6, of which 6 were waited for; matrix products, arithmetic and copies ran while one was open for 2% of the time, Pallas kernels for 0%

commit v1 on v0

v1 whole, which is shorter than its diff:
```python
import functools
import math

import jax
import jax.numpy as jnp
from jax import lax
from jax.experimental import pallas as pl
from jax.experimental.pallas import tpu as pltpu
from jax.sharding import PartitionSpec as P

MESH = pl.DeviceIdType.MESH
BF = jnp.bfloat16
F32 = jnp.float32
HD = 64
NT = 1000
NQ = 16
NS = 16
D = 3072
FR = 8
ROWS = 64
TOK = 1024
GROUP = 256
NC = 4
CW = D // NC
FS = 384
HS = 192
M1 = 2 * D // NS
M2 = 4 * D // NS


def noise_level(times):
    angle = (times / NT + 0.008) / 1.008 * (math.pi / 2)
    cosine = jnp.cos(angle)
    return 0.05 + 0.94 * cosine * cosine


def dot_nt(a, b):
    return lax.dot_general(a, b, (((1,), (1,)), ((), ())), preferred_element_type=F32)


def dot(a, b):
    return jnp.dot(a, b, preferred_element_type=F32)


def lnorm(v):
    centre = v - jnp.mean(v, -1, keepdims=True)
    spread = jnp.mean(centre * centre, -1, keepdims=True)
    return centre * lax.rsqrt(spread + 1e-05)


def kernel(
    lev, lat, noise, patch_h, tw_h, ada_h, qkv_h, out_h, up_h, down_h, proj_h,
    pred, lato,
    patch, tw, ada, qkv, proj, wo, wu, wd,
    p1, p2, rs1, rs2, mod1, mod2,
    xs, xb, xg, xet, acc_m, acc_s, abuf, mt, qt, kn, va, msend, mixt, mixa,
    res, own, s_o, s_r, s_l, p_r, p_l,
    rl1, rr1, ol1, or1, rl2, rr2, ol2, or2,
    nbuf, hacc, hid, mv, cs, cr,
    lsem, ps, pr, ys, yr, fs, fr, ms1, mr1, ms2, mr2, ms3, mr3, ms4, mr4, xss, xrs,
    as_, ar, ss1, sr1, ss2, sr2, gs, gr, csem,
):
    q = lax.axis_index("queue")
    s = lax.axis_index("space")
    core = lax.rem(s, 2)
    x = lax.rem(s // 2, 4)
    y = s // 8

    def at(y_, x_, c_):
        return (y_ * 4 + x_) * 2 + c_

    mate = at(y, x, 1 - core)
    over = at(1 - y, x, core)
    q_flip = q + 1 - 2 * lax.rem(q, 2)
    right = at(y, lax.rem(x + 1, 4), core)
    left = at(y, lax.rem(x + 3, 4), core)
    q_next = lax.rem(q + 1, NQ)
    q_prev = lax.rem(q + NQ - 1, NQ)

    def local(i, src, dst):
        return pltpu.make_async_copy(src, dst, lsem.at[i])

    def remote(src, dst, ssem, rsem, sp, qq=None):
        return pltpu.make_async_remote_copy(
            src_ref=src, dst_ref=dst, send_sem=ssem, recv_sem=rsem,
            device_id=(q if qq is None else qq, sp), device_id_type=MESH,
        )

    c_tw = local(0, tw_h, tw)
    c_ada = local(1, ada_h, ada)
    c_patch = local(2, patch_h, patch)
    c_qkv = local(3, qkv_h, qkv)
    c_wo = local(4, out_h, wo.at[pl.ds(0, HS)])
    c_wu = local(5, up_h, wu.at[:, pl.ds(0, FS)])
    c_wd = local(6, down_h, wd.at[pl.ds(0, FS)])
    c_proj = local(7, proj_h, proj)
    for c in (c_tw, c_ada, c_patch, c_qkv):
        c.start()

    bar = pltpu.get_barrier_semaphore()

    def hello(d, carry):
        pl.semaphore_signal(
            bar, inc=1, device_id=(q, lax.rem(s + d, NS)), device_id_type=MESH
        )
        return carry

    lax.fori_loop(1, NS, hello, 0)
    for dev in ((q_flip, over), (q_next, s), (q_prev, s)):
        pl.semaphore_signal(bar, inc=1, device_id=dev, device_id_type=MESH)

    row = lax.broadcasted_iota(jnp.int32, (FR, 128), 0)
    now = jnp.zeros((FR, 128), F32)
    later = jnp.zeros((FR, 128), F32)
    for f in range(FR):
        t_now = lev[f, q].astype(F32)
        if f < FR - 1:
            t_later = lev[f + 1, q].astype(F32)
        else:
            t_later = lev[0, jnp.minimum(q + 1, NQ - 1)].astype(F32)
        now = jnp.where(row == f, t_now, now)
        later = jnp.where(row == f, t_later, later)
    a_now = noise_level(now)
    a_after = noise_level(later)
    a_after = jnp.where((row == FR - 1) & (q == NQ - 1), 1.0, a_after)
    keep = jnp.sqrt(a_after / a_now)
    mix = jnp.sqrt(1.0 - a_after) - jnp.sqrt(a_after * (1.0 - a_now) / a_now)

    half = D // 2
    lane = lax.broadcasted_iota(jnp.int32, (FR, half), 1).astype(F32)
    freqs = jnp.exp(-math.log(10000.0) * lane / half)
    angle = now[:, 0:1] * freqs
    c_tw.wait()
    pre = dot_nt(jnp.cos(angle).astype(BF), tw[:, 0:half]) + dot_nt(
        jnp.sin(angle).astype(BF), tw[:, half:D]
    )
    timing = (pre * jax.nn.sigmoid(pre)).astype(BF)
    c_ada.wait()
    for k in range(2):
        p1[:, k * D : (k + 1) * D] = dot(timing, ada[k])

    c_patch.wait()
    x_own = lat[...]
    res[...] = dot(x_own.astype(BF), patch[...])
    full = res[...]
    centre = full - jnp.mean(full, -1, keepdims=True)
    spread = jnp.mean(centre * centre, -1, keepdims=True)
    rstd = lax.rsqrt(spread + 1e-05)
    r_hi = rstd.astype(BF).astype(F32)
    r_mid = (rstd - r_hi).astype(BF).astype(F32)
    r_lo = rstd - r_hi - r_mid
    xs[...] = jnp.zeros_like(xs)
    xs[:, 0:HD] = x_own
    lane_x = lax.broadcasted_iota(jnp.int32, (ROWS, 128), 1)
    packed = xs[...]
    packed = jnp.where(lane_x == 64, r_hi, packed)
    packed = jnp.where(lane_x == 65, r_mid, packed)
    packed = jnp.where(lane_x == 66, r_lo, packed)
    xb[...] = packed.astype(BF)

    def block(sp):
        return (lax.rem(sp, 2) + 2 * (sp // 8)) * 4 + lax.rem(sp // 2, 4)

    def xrows(sp):
        return pl.ds(pl.multiple_of(block(sp) * ROWS, ROWS), ROWS)

    xg[xrows(s), :] = xb[...]

    def cols(sp, width):
        return pl.ds(pl.multiple_of(sp * width, 128), width)

    pl.semaphore_wait(bar, NS + 2)

    def reduce_copy(part, recv, width, ssem, rsem, sp_to, sp_from, d):
        return remote(
            part.at[:, cols(sp_to, width)], recv.at[sp_from], ssem.at[d], rsem.at[sp_from], sp_to
        )

    def spread_copy(mod, width, ssem, rsem, sp_to, sp_from, d):
        view = mod.at[:, cols(sp_from, width)]
        return remote(view, view, ssem.at[d], rsem.at[sp_from], sp_to)

    def x_copy(sp_to, sp_from, d):
        return remote(xb, xg.at[xrows(sp_from), :], xss.at[d], xrs.at[sp_from], sp_to)

    def every(start):
        def step(d, carry):
            start(d, lax.rem(s + d, NS))
            return carry

        lax.fori_loop(1, NS, step, 0)

    every(lambda d, o: reduce_copy(p1, rs1, M1, ms1, mr1, o, s, d).start())
    every(lambda d, o: x_copy(o, s, d).start())

    w_wo = remote(out_h, wo.at[pl.ds(HS, HS)], ps.at[0], pr.at[0], mate)
    w_wu = remote(up_h, wu.at[:, pl.ds(FS, FS)], ps.at[1], pr.at[1], mate)
    w_wd = remote(down_h, wd.at[pl.ds(FS, FS)], ps.at[2], pr.at[2], mate)

    y_pairs = []
    f_copies = []

    def piece(i, source, target, forward_from, forward_to):
        pair = []
        for h, qq in ((0, None), (1, q_flip)):
            pair.append(remote(source(h), target(h), ys.at[i, h], yr.at[i, h], over, qq))
        y_pairs.append(pair)
        f_copies.append(remote(forward_from, forward_to, fs.at[i], fr.at[i], mate))

    ho = HS // 2
    piece(
        0,
        lambda h: out_h.at[pl.ds(h * ho, ho)],
        lambda h: wo.at[pl.ds(2 * HS + h * ho, ho)],
        wo.at[pl.ds(2 * HS, HS)],
        wo.at[pl.ds(3 * HS, HS)],
    )
    hu = CW // 2
    for k in range(NC):
        piece(
            1 + k,
            lambda h, k=k: up_h.at[pl.ds(k * CW + h * hu, hu)],
            lambda h, k=k: wu.at[pl.ds(k * CW + h * hu, hu), pl.ds(2 * FS, FS)],
            wu.at[pl.ds(k * CW, CW), pl.ds(2 * FS, FS)],
            wu.at[pl.ds(k * CW, CW), pl.ds(3 * FS, FS)],
        )
    hd = FS // 2
    for k in range(NC):
        piece(
            1 + NC + k,
            lambda h, k=k: down_h.at[pl.ds(h * hd, hd), pl.ds(k * CW, CW)],
            lambda h, k=k: wd.at[pl.ds(2 * FS + h * hd, hd), pl.ds(k * CW, CW)],
            wd.at[pl.ds(2 * FS, FS), pl.ds(k * CW, CW)],
            wd.at[pl.ds(3 * FS, FS), pl.ds(k * CW, CW)],
        )

    def push(i):
        for c in y_pairs[i]:
            c.start()

    def forward(i):
        for c in y_pairs[i]:
            c.wait_recv()
        f_copies[i].start()

    c_wo.start()
    w_wo.start()
    push(0)
    c_proj.start()

    for k in range(4):
        p2[:, k * D : (k + 1) * D] = dot(timing, ada[2 + k])
    every(lambda d, o: reduce_copy(p2, rs2, M2, ms2, mr2, o, s, d).start())

    def total(part, recv, mod, width, ssem, rsem):
        def add(d, acc):
            o = lax.rem(s + d, NS)
            reduce_copy(part, recv, width, ssem, rsem, s, o, d).wait_recv()
            return acc + recv[o]

        mod[:, cols(s, width)] = lax.fori_loop(1, NS, add, part[:, cols(s, width)])

    total(p1, rs1, mod1, M1, ms1, mr1)
    every(lambda d, o: spread_copy(mod1, M1, ms3, mr3, o, s, d).start())
    total(p2, rs2, mod2, M2, ms2, mr2)
    every(lambda d, o: spread_copy(mod2, M2, ms4, mr4, o, s, d).start())

    c_wu.start()
    w_wu.start()
    for k in range(NC):
        push(1 + k)

    every(lambda d, o: x_copy(s, o, d).wait_recv())
    xt = xg[...].astype(F32).T
    rstd_all = xt[64:65] + xt[65:66] + xt[66:67]
    frame = lax.rem(lax.broadcasted_iota(jnp.int32, (HD, TOK), 1), FR)
    xt = xt[0:HD]
    for f in range(FR):
        xet[f * HD : (f + 1) * HD, :] = jnp.where(frame == f, xt, 0.0).astype(BF)
    hot = (
        lax.rem(lax.broadcasted_iota(jnp.int32, (16, TOK), 1), FR)
        == lax.rem(lax.broadcasted_iota(jnp.int32, (16, TOK), 0), FR)
    ).astype(F32).astype(BF)

    every(lambda d, o: spread_copy(mod1, M1, ms3, mr3, s, o, d).wait_recv())
    c_qkv.wait()
    acc_m[...] = jnp.zeros_like(acc_m)
    acc_s[...] = jnp.zeros_like(acc_s)
    mean_w = jnp.mean(patch[...].astype(F32), -1, keepdims=True)

    def fold(j, carry):
        c = pl.ds(pl.multiple_of(j * CW, 128), CW)
        centred = patch[:, c].astype(F32) - mean_w
        gain = 1.0 + mod1[:, pl.ds(pl.multiple_of(D + j * CW, 128), CW)]
        for f in range(FR):
            abuf[f * HD : (f + 1) * HD, :] = (centred * gain[f : f + 1]).astype(BF)
        shift = mod1[:, c]
        hi = shift.astype(BF).astype(F32)
        both = jnp.concatenate([hi, shift - hi], 0).astype(BF)
        w = qkv[:, c]
        acc_m[...] += dot_nt(w, abuf[...])
        acc_s[...] += dot_nt(w, both)
        return carry

    lax.fori_loop(0, NC, fold, 0)
    mt[...] = acc_m[...].astype(BF)
    s_hi = acc_s[...].astype(BF)
    s_lo = (acc_s[...] - s_hi.astype(F32)).astype(BF)

    def project(k):
        r = slice(k * HS, (k + 1) * HS)
        out = dot(mt[r, :], xet[...]) * rstd_all
        return (out + dot(s_hi[r], hot) + dot(s_lo[r], hot)).reshape(3, HD, TOK)

    def head_norm(v):
        centre = v - jnp.mean(v, 1, keepdims=True)
        spread = jnp.mean(centre * centre, 1, keepdims=True)
        return centre * lax.rsqrt(spread + 1e-06)

    queries = head_norm(project(0)) * (HD**-0.5 / math.log(2.0))
    qt[...] = queries.astype(BF)
    keys = head_norm(project(1))
    for h in range(3):
        kn[h] = keys[h].T.astype(BF)
    values = project(2)
    for h in range(3):
        va[h, 0:HD, :] = values[h].astype(BF)
        va[h, HD : HD + 16, :] = jnp.ones((16, TOK), BF)

    def group_rows(slot):
        y_ = lax.rem(y + slot // 2, 2)
        c_ = lax.rem(core + slot, 2)
        return y_, c_

    def mix_copy(slot):
        y_, c_ = group_rows(slot)
        return remote(msend.at[slot], mixt.at[slot], as_.at[slot], ar.at[slot], at(y_, x, c_))

    def attend(i, carry):
        slot = 3 - i
        y_, c_ = group_rows(slot)
        g = pl.ds(pl.multiple_of((y_ * 2 + c_) * GROUP, GROUP), GROUP)
        for h in range(3):
            scores = dot(kn[h], qt[h, :, g])
            weights = jnp.exp2(scores).astype(BF)
            o = dot(va[h], weights)
            msend[slot, h * HD : (h + 1) * HD, :] = (o[0:HD] / o[HD : HD + 1]).astype(BF)

        @pl.when(slot > 0)
        def _():
            mix_copy(slot).start()

        return carry

    lax.fori_loop(0, 4, attend, 0)

    def turn(slot, src):
        v = src.astype(F32).T.astype(BF)
        for b in range(4):
            o = lax.rem(b - x + 4, 4)
            r = pl.ds(pl.multiple_of(o * ROWS, ROWS), ROWS)
            mixa[slot, r, :] = v[b * ROWS : (b + 1) * ROWS]

    turn(0, msend[0])
    forward(0)
    for slot in range(1, 4):
        mix_copy(slot).wait_recv()
        turn(slot, mixt[slot])
    c_wo.wait()
    w_wo.wait_recv()
    f_copies[0].wait_recv()

    def chunk(j):
        return pl.ds(pl.multiple_of(j * CW, 128), CW)

    lo, hi32 = pl.ds(0, 32), pl.ds(32, 32)

    def sum_phase(term, rl, rr, ol, or_, ss, sr):
        def sends(j):
            c = chunk(j)
            return dict(
                o_r=remote(s_o.at[lo, c], ol.at[:, c], ss.at[0, j], sr.at[0, j], right),
                o_l=remote(s_o.at[hi32, c], or_.at[:, c], ss.at[1, j], sr.at[1, j], left),
                d_r=remote(s_r.at[hi32, c], rl.at[hi32, c], ss.at[2, j], sr.at[2, j], right),
                d_l=remote(s_l.at[lo, c], rr.at[lo, c], ss.at[3, j], sr.at[3, j], left),
                a_r=remote(s_r.at[lo, c], rl.at[lo, c], ss.at[4, j], sr.at[4, j], right),
                a_l=remote(s_l.at[hi32, c], rr.at[hi32, c], ss.at[5, j], sr.at[5, j], left),
            )

        def passed(j):
            c = chunk(j)
            m = sends(j)
            m["o_r"].wait_recv()
            s_r[0:32, c] = (p_r[:, c] + ol[:, c].astype(F32)).astype(BF)
            m["a_r"].start()
            m["o_l"].wait_recv()
            s_l[32:64, c] = (p_l[:, c] + or_[:, c].astype(F32)).astype(BF)
            m["a_l"].start()

        def step(j, carry):
            c = chunk(j)
            v = term(c)
            m = sends(j)
            s_o[:, c] = v[128:192].astype(BF)
            m["o_r"].start()
            m["o_l"].start()
            s_r[32:64, c] = v[96:128].astype(BF)
            m["d_r"].start()
            s_l[0:32, c] = v[192:224].astype(BF)
            m["d_l"].start()
            p_r[:, c] = v[64:96]
            p_l[:, c] = v[224:256]
            own[:, c] = v[0:64]

            @pl.when(j > 0)
            def _():
                passed(j - 1)

            return carry

        lax.fori_loop(0, NC, step, 0)
        passed(NC - 1)

        def finish(j, carry):
            m = sends(j)
            for key in ("d_r", "d_l", "a_r", "a_l"):
                m[key].wait_recv()
            return carry

        lax.fori_loop(0, NC, finish, 0)

        def sent(j, carry):
            for c in sends(j).values():
                c.wait_send()
            return carry

        return lambda: lax.fori_loop(0, NC, sent, 0)

    def out_term(c):
        acc = dot(mixa[0], wo[0:HS, c])
        for slot in range(1, 4):
            acc += dot(mixa[slot], wo[slot * HS : (slot + 1) * HS, c])
        return acc

    sent1 = sum_phase(out_term, rl1, rr1, ol1, or1, ss1, sr1)

    c_wd.start()
    w_wd.start()
    for k in range(NC):
        push(1 + NC + k)

    every(lambda d, o: spread_copy(mod2, M2, ms4, mr4, s, o, d).wait_recv())

    def update(i, rl, rr, gate):
        r = pl.ds(pl.multiple_of(i * 16, 16), 16)
        summed = own[r, :] + rl[r, :].astype(F32) + rr[r, :].astype(F32)
        new = res[r, :].reshape(2, FR, D) + mod2[:, gate * D : (gate + 1) * D] * summed.reshape(2, FR, D)
        return r, new

    def second(i, carry):
        r, new = update(i, rl1, rr1, 0)
        res[r, :] = new.reshape(16, D)
        v = lnorm(new) * (1.0 + mod2[:, 2 * D : 3 * D]) + mod2[:, D : 2 * D]
        nbuf[r, :] = v.reshape(16, D).astype(BF)
        return carry

    lax.fori_loop(0, ROWS // 16, second, 0)

    def gathers(j):
        c = chunk(j)

        def go(i, src, dst, dev):
            return remote(
                nbuf.at[pl.ds(src, 32), c], nbuf.at[pl.ds(dst, 32), c], gs.at[i, j], gr.at[i, j], dev
            )

        return [
            go(0, 0, 192, right),
            go(1, 32, 96, left),
            go(2, 32, 224, right),
            go(3, 0, 64, left),
            go(4, 192, 128, right),
            go(5, 96, 160, left),
        ]

    def open_gather(j, carry):
        for c in gathers(j)[:4]:
            c.start()
        return carry

    lax.fori_loop(0, NC, open_gather, 0)

    def relay(j):
        m = gathers(j)
        m[0].wait_recv()
        m[4].start()
        m[1].wait_recv()
        m[5].start()

    hacc[...] = jnp.zeros_like(hacc)
    for k in range(NC):
        forward(1 + k)
    relay(0)
    c_wu.wait()
    w_wu.wait_recv()

    for j in range(NC):
        if j + 1 < NC:
            relay(j + 1)
        m = gathers(j)
        for i in range(2, 6):
            m[i].wait_recv()
        f_copies[1 + j].wait_recv()

        def widen(n, carry, j=j):
            c = pl.ds(pl.multiple_of(n * 512, 512), 512)
            hacc[:, c] += dot(nbuf[:, j * CW : (j + 1) * CW], wu[j * CW : (j + 1) * CW, c])
            return carry

        lax.fori_loop(0, 3, widen, 0)

    def activate(i, carry):
        r = pl.ds(pl.multiple_of(i * 16, 16), 16)
        hid[r, :] = jax.nn.gelu(hacc[r, :], approximate=True).astype(BF)
        return carry

    lax.fori_loop(0, GROUP // 16, activate, 0)
    for k in range(NC):
        forward(1 + NC + k)
    c_wd.wait()
    w_wd.wait_recv()
    for k in range(NC):
        f_copies[1 + NC + k].wait_recv()
    sent1()

    sent2 = sum_phase(lambda c: dot(hid[...], wd[:, c]), rl2, rr2, ol2, or2, ss2, sr2)

    def last(i, carry):
        r, new = update(i, rl2, rr2, 3)
        abuf_row = lnorm(new).reshape(16, D)
        for k in range(NC):
            s_o[r, k * CW : (k + 1) * CW] = abuf_row[:, k * CW : (k + 1) * CW].astype(BF)
        return carry

    sent2()
    lax.fori_loop(0, ROWS // 16, last, 0)
    c_proj.wait()
    out = dot_nt(s_o[...], proj[...])
    pred[...] = out
    moved = keep[:, 0:HD] * lat[...].reshape(FR, FR, HD) + mix[:, 0:HD] * out.reshape(FR, FR, HD)
    mv[...] = jnp.zeros_like(mv)
    mv[:, 0:HD] = moved.reshape(ROWS, HD)
    cs[...] = mv[pl.ds(FR - 1, FR, stride=FR), :]
    carry_copy = remote(cs, cr, csem.at[0], csem.at[1], s, q_next)
    carry_copy.start()
    for f in range(1, FR):
        lato[pl.ds(f, FR, stride=FR), :] = mv[pl.ds(f - 1, FR, stride=FR), :][:, 0:HD]

    every(lambda d, o: reduce_copy(p1, rs1, M1, ms1, mr1, o, s, d).wait_send())
    every(lambda d, o: reduce_copy(p2, rs2, M2, ms2, mr2, o, s, d).wait_send())
    every(lambda d, o: spread_copy(mod1, M1, ms3, mr3, o, s, d).wait_send())
    every(lambda d, o: spread_copy(mod2, M2, ms4, mr4, o, s, d).wait_send())
    every(lambda d, o: x_copy(o, s, d).wait_send())
    for slot in range(1, 4):
        mix_copy(slot).wait_send()
    for c in (w_wo, w_wu, w_wd):
        c.wait_send()
    for pair in y_pairs:
        for c in pair:
            c.wait_send()
    for c in f_copies:
        c.wait_send()

    def gathered(j, carry):
        for c in gathers(j):
            c.wait_send()
        return carry

    lax.fori_loop(0, NC, gathered, 0)
    carry_copy.wait()
    lato[pl.ds(0, FR, stride=FR), :] = jnp.where(q == 0, noise[...], cr[:, 0:HD])


def scratch():
    v = pltpu.VMEM
    dma = pltpu.SemaphoreType.DMA
    return [
        v((HD, D), BF), v((32, D), BF), v((6, 32, D), BF), v((3 * HS, D), BF), v((HD, D), BF),
        v((4 * HS, D), BF), v((D, 4 * FS), BF), v((4 * FS, D), BF),
        v((FR, 2 * D), F32), v((FR, 4 * D), F32), v((NS, FR, M1), F32), v((NS, FR, M2), F32),
        v((FR, 2 * D), F32), v((FR, 4 * D), F32),
        v((ROWS, 128), F32), v((ROWS, 128), BF), v((TOK, 128), BF), v((FR * HD, TOK), BF),
        v((3 * HS, FR * HD), F32), v((3 * HS, 16), F32), v((FR * HD, CW), BF),
        v((3 * HS, FR * HD), BF),
        v((3, HD, TOK), BF), v((3, TOK, HD), BF), v((3, HD + 16, TOK), BF),
        v((4, HS, GROUP), BF), v((4, HS, GROUP), BF), v((4, GROUP, HS), BF),
        v((ROWS, D), F32), v((ROWS, D), F32), v((ROWS, D), BF), v((ROWS, D), BF), v((ROWS, D), BF),
        v((32, D), F32), v((32, D), F32),
        v((ROWS, D), BF), v((ROWS, D), BF), v((32, D), BF), v((32, D), BF),
        v((ROWS, D), BF), v((ROWS, D), BF), v((32, D), BF), v((32, D), BF),
        v((GROUP, D), BF), v((GROUP, 4 * FS), F32), v((GROUP, 4 * FS), BF),
        v((ROWS, 128), F32), v((FR, 128), F32), v((FR, 128), F32),
        dma((8,)), dma((3,)), dma((3,)), dma((9, 2)), dma((9, 2)), dma((9,)), dma((9,)),
        dma((NS,)), dma((NS,)), dma((NS,)), dma((NS,)), dma((NS,)), dma((NS,)), dma((NS,)), dma((NS,)),
        dma((NS,)), dma((NS,)),
        dma((4,)), dma((4,)),
        dma((6, NC)), dma((6, NC)), dma((6, NC)), dma((6, NC)), dma((6, NC)), dma((6, NC)),
        dma((2,)),
    ]


def body(
    latents, fresh_noise, levels, patch_weight, time_weight, adaln_weight, qkv_weight,
    out_weight, up_weight, down_weight, proj_weight,
):
    vm = pl.BlockSpec(memory_space=pltpu.VMEM)
    hbm = pl.BlockSpec(memory_space=pl.ANY)
    pred, lato = pl.pallas_call(
        kernel,
        out_shape=(
            jax.ShapeDtypeStruct((ROWS, HD), F32),
            jax.ShapeDtypeStruct((ROWS, HD), F32),
        ),
        in_specs=[pl.BlockSpec(memory_space=pltpu.SMEM), vm, vm] + [hbm] * 8,
        out_specs=(vm, vm),
        scratch_shapes=scratch(),
        compiler_params=pltpu.CompilerParams(
            collective_id=0, has_side_effects=True, vmem_limit_bytes=60 * 1024 * 1024
        ),
    )(
        levels.T,
        latents.reshape(ROWS, HD),
        fresh_noise.reshape(FR, HD),
        patch_weight,
        time_weight.T,
        jnp.transpose(adaln_weight, (1, 0, 2)),
        jnp.transpose(qkv_weight, (1, 2, 0)).reshape(3 * HS, D),
        out_weight,
        up_weight,
        down_weight,
        proj_weight.T,
    )
    return lato.reshape(1, 8, FR, HD), pred.reshape(1, 1, 8, FR, HD)


def solution(mesh):
    in_specs = (
        P("queue", "space", None, None),
        P(None, "space", None),
        P(),
        P(),
        P(None, "space"),
        P("space", None, None),
        P(None, None, "space"),
        P("space", None),
        P(None, "space"),
        P("space", None),
        P(),
    )
    out_specs = (P("queue", "space", None, None), P(None, "queue", "space", None, None))
    return jax.shard_map(body, mesh=mesh, in_specs=in_specs, out_specs=out_specs, check_vma=False)
```

time: 432 us -> 143 us (0.33); the launches traced: 426 us -> 143 us
  waiting for transfers between devices: 354 us -> 0 us
  Pallas kernels: 0 us -> 140 us
  matrix products: 31.9 us -> 0 us
  other arithmetic: 16.4 us -> 0 us
  between operations: 14 us -> 0.64 us
  starting transfers between devices: 4.72 us -> 0 us
    pallas_call x0 -> x1, Pallas kernels: none -> 140 us  [body(): pl.pallas_call(kernel, out_shape=(jax.ShapeDtypeStruct((ROWS, HD), F32),...]
    reduce_scatter x2 -> x0, waiting for transfers between devices: 134 us -> none  [the longest x1 70.2 us: queue_turn(): lax.psum_scatter(jnp.dot(mixed, out_weight, preferred_element_type=jnp.fl...]
    psum x1 -> x0, waiting for transfers between devices: 122 us -> none  [body(): modulation = lax.psum(partial_terms, 'space')]
    all_gather x2 -> x0, waiting for transfers between devices: 96.7 us -> none  [the longest x1 49.3 us: queue_turn(): piece = lax.all_gather(normed, 'space', axis=0, tiled=True)]
    dot_general x8 -> x0, matrix products: 31.9 us -> none  [the longest x1 12 us: queue_turn(): jnp.dot(flat_hidden, down_weight, preferred_element_type=jnp.float32)]
    reduce_sum x7 -> x0, other arithmetic: 5.43 us -> none  [the longest x3 3.23 us: layer_norm(): centre = values - jnp.mean(values, -1, keepdims=True)]
    ppermute x1 -> x0, starting transfers between devices: 4.34 us -> none  [shifted(): return lax.ppermute(block, axis, route)]
  transfers between devices with their start and end apart: 6 -> 0, of which waited for: 6 -> 0; matrix products, arithmetic and copies ran while one was open for 2% -> 0% of each run, Pallas kernels for 0% -> 0%
where the time goes in v1:
time: 143 us
  Pallas kernels  140 us (98%)
  local copies, waits for them, and re-layouts  2.75 us (2%)
    pallas_call x1, Pallas kernels, body(): pl.pallas_call(kernel, out_shape=(jax.ShapeDtypeStruct((ROWS, HD), F32),...  140 us

profile of v1, /device:TPU:1, one launch (start us, length us, event | category | flops | bytes accessed | tf_op | source)
XLA Modules:
  0.0 143.2 jit_solution(1229213767221755217)
XLA Ops:
  0.6 139.8 %shard_map.122 = (f32[64,64]{1,0:T(8,128)}, f32[64,64]{1,0:T(8,128)}) custom-call(s32[8,16]{1,0:T(8,128)} %bitcast.18, f32[64,64]{1,0:T(8,128)} %bitcast.15, f32[8,64]{1,0:T(8,128)} %bitcast.19, bf16[64,3072]{1,0:T(8,128)(2,1)} %patch_h.1, bf16[32,3072]{1,0:T(8,128)(2,1)} %bitcast.14, bf16[6,32,3072]{2,1,0:T(8,128)(2,1)} %bitcast.12, ...), custom_call_target="tpu_custom_call" | custom-call | tf_op jit(solution)/shard_map/pallas_call | solution.py:618
  140.4 1.4 copy.15
  141.8 1.4 copy.16

commit v2 on v1

--- a/solution.py
+++ b/solution.py
@@ -24,8 +24,8 @@
 CW = D // NC
 FS = 384
 HS = 192
-M1 = 2 * D // NS
-M2 = 4 * D // NS
+M1 = 2 * D // 8
+M2 = 4 * D // 8
 
 
 def noise_level(times):
@@ -52,12 +52,12 @@
     lev, lat, noise, patch_h, tw_h, ada_h, qkv_h, out_h, up_h, down_h, proj_h,
     pred, lato,
     patch, tw, ada, qkv, proj, wo, wu, wd,
-    p1, p2, rs1, rs2, mod1, mod2,
-    xs, xb, xg, xet, acc_m, acc_s, abuf, mt, qt, kn, va, msend, mixt, mixa,
+    p1, p2, ra1, ra2, rb1, rb2, b1, b2, t1, t2, mod1, mod2,
+    xs, xg, xet, acc_m, acc_s, abuf, mt, qt, kn, va, msend, mixt, mixa,
     res, own, s_o, s_r, s_l, p_r, p_l,
     rl1, rr1, ol1, or1, rl2, rr2, ol2, or2,
     nbuf, hacc, hid, mv, cs, cr,
-    lsem, ps, pr, ys, yr, fs, fr, ms1, mr1, ms2, mr2, ms3, mr3, ms4, mr4, xss, xrs,
+    lsem, ps, pr, ys, yr, zs, zr, fs, fr, mss, msr, xss, xrs,
     as_, ar, ss1, sr1, ss2, sr2, gs, gr, csem,
 ):
     q = lax.axis_index("queue")
@@ -99,14 +99,14 @@
 
     bar = pltpu.get_barrier_semaphore()
 
-    def hello(d, carry):
-        pl.semaphore_signal(
-            bar, inc=1, device_id=(q, lax.rem(s + d, NS)), device_id_type=MESH
-        )
-        return carry
-
-    lax.fori_loop(1, NS, hello, 0)
-    for dev in ((q_flip, over), (q_next, s), (q_prev, s)):
+    group = ((mate, 1), (over, 2), (at(1 - y, x, 1 - core), 3))
+    ring = ((right, 1), (at(y, lax.rem(x + 2, 4), core), 2), (left, 3))
+    par = lax.rem(q // 2, 2)
+    z_to = [lax.rem(q + NQ + 2 * (1 - 2 * par) * (1 - 2 * h), NQ) for h in range(2)]
+    for dev in (
+        [(q, o) for o, _ in group + ring]
+        + [(q_flip, over), (q_next, s), (q_prev, s), (z_to[0], s), (z_to[1], s)]
+    ):
         pl.semaphore_signal(bar, inc=1, device_id=dev, device_id_type=MESH)
 
     row = lax.broadcasted_iota(jnp.int32, (FR, 128), 0)
@@ -137,7 +137,10 @@
     timing = (pre * jax.nn.sigmoid(pre)).astype(BF)
     c_ada.wait()
     for k in range(2):
-        p1[:, k * D : (k + 1) * D] = dot(timing, ada[k])
+        part = dot(timing, ada[k])
+        for h in range(2):
+            two = [part[:, (2 * h + i) * M1 : (2 * h + i + 1) * M1] for i in range(2)]
+            p1[2 * k + h] = jnp.concatenate(two, 0).astype(BF)
 
     c_patch.wait()
     x_own = lat[...]
@@ -156,122 +159,159 @@
     packed = jnp.where(lane_x == 64, r_hi, packed)
     packed = jnp.where(lane_x == 65, r_mid, packed)
     packed = jnp.where(lane_x == 66, r_lo, packed)
-    xb[...] = packed.astype(BF)
-
-    def block(sp):
-        return (lax.rem(sp, 2) + 2 * (sp // 8)) * 4 + lax.rem(sp // 2, 4)
-
-    def xrows(sp):
-        return pl.ds(pl.multiple_of(block(sp) * ROWS, ROWS), ROWS)
-
-    xg[xrows(s), :] = xb[...]
-
-    def cols(sp, width):
-        return pl.ds(pl.multiple_of(sp * width, 128), width)
-
-    pl.semaphore_wait(bar, NS + 2)
-
-    def reduce_copy(part, recv, width, ssem, rsem, sp_to, sp_from, d):
-        return remote(
-            part.at[:, cols(sp_to, width)], recv.at[sp_from], ssem.at[d], rsem.at[sp_from], sp_to
-        )
-
-    def spread_copy(mod, width, ssem, rsem, sp_to, sp_from, d):
-        view = mod.at[:, cols(sp_from, width)]
-        return remote(view, view, ssem.at[d], rsem.at[sp_from], sp_to)
-
-    def x_copy(sp_to, sp_from, d):
-        return remote(xb, xg.at[xrows(sp_from), :], xss.at[d], xrs.at[sp_from], sp_to)
-
-    def every(start):
-        def step(d, carry):
-            start(d, lax.rem(s + d, NS))
-            return carry
-
-        lax.fori_loop(1, NS, step, 0)
-
-    every(lambda d, o: reduce_copy(p1, rs1, M1, ms1, mr1, o, s, d).start())
-    every(lambda d, o: x_copy(o, s, d).start())
+    me4 = y * 2 + core
+    xg[x, me4] = packed.astype(BF)
+
+    pl.semaphore_wait(bar, 11)
+
+    def slot_of(slot):
+        return lax.rem(y + slot // 2, 2) * 2 + lax.rem(core + slot, 2)
+
+    def group_sum(k, part, recv):
+        ssem, rsem = mss.at[0, k], msr.at[0, k]
+        return [
+            remote(part.at[slot_of(i)], recv.at[i], ssem.at[i], rsem.at[i], o) for o, i in group
+        ]
+
+    def ring_sum(k, mine, recv):
+        ssem, rsem = mss.at[1, k], msr.at[1, k]
+        return [remote(mine, recv.at[i], ssem.at[i], rsem.at[i], o) for o, i in ring]
+
+    def group_spread(k, tot):
+        ssem, rsem = mss.at[2, k], msr.at[2, k]
+        return [
+            remote(tot.at[me4], tot.at[me4], ssem.at[i], rsem.at[i], o) for o, i in group
+        ]
+
+    x_near = [
+        remote(xg.at[x, me4], xg.at[x, me4], xss.at[0, i], xrs.at[0, i], o) for o, i in group
+    ]
+    x_far = [remote(xg.at[x], xg.at[x], xss.at[1, i], xrs.at[1, i], o) for o, i in ring]
+
+    def begin(copies):
+        for c in copies:
+            c.start()
+
+    def arrive(copies):
+        for c in copies:
+            c.wait_recv()
+
+    steps = []
+    for k, (part, ra, mine, rb, tot) in enumerate(((p1, ra1, b1, rb1, t1), (p2, ra2, b2, rb2, t2))):
+        steps.append((group_sum(k, part, ra), ring_sum(k, mine, rb), group_spread(k, tot)))
+
+    def join(k):
+        part, ra, mine = ((p1, ra1, b1), (p2, ra2, b2))[k]
+        arrive(steps[k][0])
+        acc = part[me4].astype(F32)
+        for i in range(1, 4):
+            acc += ra[i].astype(F32)
+        mine[...] = acc.astype(BF)
+        begin(steps[k][1])
+
+    def close(k):
+        mine, rb, tot = ((b1, rb1, t1), (b2, rb2, t2))[k]
+        arrive(steps[k][1])
+        acc = mine[...].astype(F32)
+        for i in range(1, 4):
+            acc += rb[i].astype(F32)
+        tot[me4] = acc.astype(BF)
+        begin(steps[k][2])
+
+    def unpack(k):
+        tot, mod, w = ((t1, mod1, M1), (t2, mod2, M2))[k]
+        arrive(steps[k][2])
+        for m in range(4):
+            v = tot[m].astype(F32)
+            mod[:, 2 * m * w : (2 * m + 1) * w] = v[0:FR]
+            mod[:, (2 * m + 1) * w : (2 * m + 2) * w] = v[FR : 2 * FR]
+
+    begin(steps[0][0])
+    begin(x_near)
 
     w_wo = remote(out_h, wo.at[pl.ds(HS, HS)], ps.at[0], pr.at[0], mate)
     w_wu = remote(up_h, wu.at[:, pl.ds(FS, FS)], ps.at[1], pr.at[1], mate)
     w_wd = remote(down_h, wd.at[pl.ds(FS, FS)], ps.at[2], pr.at[2], mate)
 
     y_pairs = []
+    z_sends = []
+    z_recvs = []
     f_copies = []
 
     def piece(i, source, target, forward_from, forward_to):
-        pair = []
-        for h, qq in ((0, None), (1, q_flip)):
-            pair.append(remote(source(h), target(h), ys.at[i, h], yr.at[i, h], over, qq))
-        y_pairs.append(pair)
+        mine = [2 * par + h for h in range(2)]
+        theirs = [2 * (1 - par) + h for h in range(2)]
+        y_pairs.append([
+            remote(source(mine[h]), target(mine[h]), ys.at[i, h], yr.at[i, h], over, (q, q_flip)[h])
+            for h in range(2)
+        ])
+        for lst, parts in ((z_sends, mine), (z_recvs, theirs)):
+            lst.append([
+                remote(target(parts[h]), target(parts[h]), zs.at[i, h], zr.at[i, h], s, z_to[h])
+                for h in range(2)
+            ])
         f_copies.append(remote(forward_from, forward_to, fs.at[i], fr.at[i], mate))
 
-    ho = HS // 2
+    def rows_of(base, part, size):
+        return pl.ds(pl.multiple_of(base + part * size, 16), size)
+
     piece(
         0,
-        lambda h: out_h.at[pl.ds(h * ho, ho)],
-        lambda h: wo.at[pl.ds(2 * HS + h * ho, ho)],
+        lambda p: out_h.at[rows_of(0, p, HS // 4)],
+        lambda p: wo.at[rows_of(2 * HS, p, HS // 4)],
         wo.at[pl.ds(2 * HS, HS)],
         wo.at[pl.ds(3 * HS, HS)],
     )
-    hu = CW // 2
     for k in range(NC):
         piece(
             1 + k,
-            lambda h, k=k: up_h.at[pl.ds(k * CW + h * hu, hu)],
-            lambda h, k=k: wu.at[pl.ds(k * CW + h * hu, hu), pl.ds(2 * FS, FS)],
+            lambda p, k=k: up_h.at[rows_of(k * CW, p, CW // 4)],
+            lambda p, k=k: wu.at[rows_of(k * CW, p, CW // 4), pl.ds(2 * FS, FS)],
             wu.at[pl.ds(k * CW, CW), pl.ds(2 * FS, FS)],
             wu.at[pl.ds(k * CW, CW), pl.ds(3 * FS, FS)],
         )
-    hd = FS // 2
     for k in range(NC):
         piece(
             1 + NC + k,
-            lambda h, k=k: down_h.at[pl.ds(h * hd, hd), pl.ds(k * CW, CW)],
-            lambda h, k=k: wd.at[pl.ds(2 * FS + h * hd, hd), pl.ds(k * CW, CW)],
+            lambda p, k=k: down_h.at[rows_of(0, p, FS // 4), pl.ds(k * CW, CW)],
+            lambda p, k=k: wd.at[rows_of(2 * FS, p, FS // 4), pl.ds(k * CW, CW)],
             wd.at[pl.ds(2 * FS, FS), pl.ds(k * CW, CW)],
             wd.at[pl.ds(3 * FS, FS), pl.ds(k * CW, CW)],
         )
 
     def push(i):
-        for c in y_pairs[i]:
-            c.start()
+        begin(y_pairs[i])
+
+    def along(i):
+        arrive(y_pairs[i])
+        begin(z_sends[i])
 
     def forward(i):
-        for c in y_pairs[i]:
-            c.wait_recv()
+        arrive(z_recvs[i])
         f_copies[i].start()
 
     c_wo.start()
     w_wo.start()
+    c_proj.start()
+
+    for k in range(4):
+        part = dot(timing, ada[2 + k])
+        p2[k] = jnp.concatenate([part[:, 0:M2], part[:, M2 : 2 * M2]], 0).astype(BF)
+    begin(steps[1][0])
+    join(0)
+    arrive(x_near)
+    begin(x_far)
+    join(1)
+    close(0)
     push(0)
-    c_proj.start()
-
-    for k in range(4):
-        p2[:, k * D : (k + 1) * D] = dot(timing, ada[2 + k])
-    every(lambda d, o: reduce_copy(p2, rs2, M2, ms2, mr2, o, s, d).start())
-
-    def total(part, recv, mod, width, ssem, rsem):
-        def add(d, acc):
-            o = lax.rem(s + d, NS)
-            reduce_copy(part, recv, width, ssem, rsem, s, o, d).wait_recv()
-            return acc + recv[o]
-
-        mod[:, cols(s, width)] = lax.fori_loop(1, NS, add, part[:, cols(s, width)])
-
-    total(p1, rs1, mod1, M1, ms1, mr1)
-    every(lambda d, o: spread_copy(mod1, M1, ms3, mr3, o, s, d).start())
-    total(p2, rs2, mod2, M2, ms2, mr2)
-    every(lambda d, o: spread_copy(mod2, M2, ms4, mr4, o, s, d).start())
-
+    close(1)
     c_wu.start()
     w_wu.start()
-    for k in range(NC):
-        push(1 + k)
-
-    every(lambda d, o: x_copy(s, o, d).wait_recv())
-    xt = xg[...].astype(F32).T
+    push(1)
+    push(2)
+
+    arrive(x_far)
+    xt = jnp.concatenate([xg[b, m] for m in range(4) for b in range(4)], 0).astype(F32).T
     rstd_all = xt[64:65] + xt[65:66] + xt[66:67]
     frame = lax.rem(lax.broadcasted_iota(jnp.int32, (HD, TOK), 1), FR)
     xt = xt[0:HD]
@@ -282,7 +322,7 @@
         == lax.rem(lax.broadcasted_iota(jnp.int32, (16, TOK), 0), FR)
     ).astype(F32).astype(BF)
 
-    every(lambda d, o: spread_copy(mod1, M1, ms3, mr3, s, o, d).wait_recv())
+    unpack(0)
     c_qkv.wait()
     acc_m[...] = jnp.zeros_like(acc_m)
     acc_s[...] = jnp.zeros_like(acc_s)
@@ -303,6 +343,9 @@
         return carry
 
     lax.fori_loop(0, NC, fold, 0)
+    along(0)
+    push(3)
+    push(4)
     mt[...] = acc_m[...].astype(BF)
     s_hi = acc_s[...].astype(BF)
     s_lo = (acc_s[...] - s_hi.astype(F32)).astype(BF)
@@ -327,6 +370,9 @@
         va[h, 0:HD, :] = values[h].astype(BF)
         va[h, HD : HD + 16, :] = jnp.ones((16, TOK), BF)
 
+    along(1)
+    along(2)
+
     def group_rows(slot):
         y_ = lax.rem(y + slot // 2, 2)
         c_ = lax.rem(core + slot, 2)
@@ -366,6 +412,12 @@
     for slot in range(1, 4):
         mix_copy(slot).wait_recv()
         turn(slot, mixt[slot])
+    c_wd.start()
+    w_wd.start()
+    for k in range(NC):
+        push(1 + NC + k)
+    along(3)
+    along(4)
     c_wo.wait()
     w_wo.wait_recv()
     f_copies[0].wait_recv()
@@ -444,12 +496,8 @@
 
     sent1 = sum_phase(out_term, rl1, rr1, ol1, or1, ss1, sr1)
 
-    c_wd.start()
-    w_wd.start()
-    for k in range(NC):
-        push(1 + NC + k)
-
-    every(lambda d, o: spread_copy(mod2, M2, ms4, mr4, s, o, d).wait_recv())
+
+    unpack(1)
 
     def update(i, rl, rr, gate):
         r = pl.ds(pl.multiple_of(i * 16, 16), 16)
@@ -500,6 +548,7 @@
     hacc[...] = jnp.zeros_like(hacc)
     for k in range(NC):
         forward(1 + k)
+        along(1 + NC + k)
     relay(0)
     c_wu.wait()
     w_wu.wait_recv()
@@ -556,16 +605,13 @@
     for f in range(1, FR):
         lato[pl.ds(f, FR, stride=FR), :] = mv[pl.ds(f - 1, FR, stride=FR), :][:, 0:HD]
 
-    every(lambda d, o: reduce_copy(p1, rs1, M1, ms1, mr1, o, s, d).wait_send())
-    every(lambda d, o: reduce_copy(p2, rs2, M2, ms2, mr2, o, s, d).wait_send())
-    every(lambda d, o: spread_copy(mod1, M1, ms3, mr3, o, s, d).wait_send())
-    every(lambda d, o: spread_copy(mod2, M2, ms4, mr4, o, s, d).wait_send())
-    every(lambda d, o: x_copy(o, s, d).wait_send())
+    for c in sum((list(t) for p in steps for t in p), x_near + x_far):
+        c.wait_send()
     for slot in range(1, 4):
         mix_copy(slot).wait_send()
     for c in (w_wo, w_wu, w_wd):
         c.wait_send()
-    for pair in y_pairs:
+    for pair in y_pairs + z_sends:
         for c in pair:
             c.wait_send()
     for c in f_copies:
@@ -587,9 +633,10 @@
     return [
         v((HD, D), BF), v((32, D), BF), v((6, 32, D), BF), v((3 * HS, D), BF), v((HD, D), BF),
         v((4 * HS, D), BF), v((D, 4 * FS), BF), v((4 * FS, D), BF),
-        v((FR, 2 * D), F32), v((FR, 4 * D), F32), v((NS, FR, M1), F32), v((NS, FR, M2), F32),
-        v((FR, 2 * D), F32), v((FR, 4 * D), F32),
-        v((ROWS, 128), F32), v((ROWS, 128), BF), v((TOK, 128), BF), v((FR * HD, TOK), BF),
+        v((4, 16, M1), BF), v((4, 16, M2), BF), v((4, 16, M1), BF), v((4, 16, M2), BF),
+        v((4, 16, M1), BF), v((4, 16, M2), BF), v((16, M1), BF), v((16, M2), BF),
+        v((4, 16, M1), BF), v((4, 16, M2), BF), v((FR, 2 * D), F32), v((FR, 4 * D), F32),
+        v((ROWS, 128), F32), v((4, 4, ROWS, 128), BF), v((FR * HD, TOK), BF),
         v((3 * HS, FR * HD), F32), v((3 * HS, 16), F32), v((FR * HD, CW), BF),
         v((3 * HS, FR * HD), BF),
         v((3, HD, TOK), BF), v((3, TOK, HD), BF), v((3, HD + 16, TOK), BF),
@@ -600,9 +647,8 @@
         v((ROWS, D), BF), v((ROWS, D), BF), v((32, D), BF), v((32, D), BF),
         v((GROUP, D), BF), v((GROUP, 4 * FS), F32), v((GROUP, 4 * FS), BF),
         v((ROWS, 128), F32), v((FR, 128), F32), v((FR, 128), F32),
-        dma((8,)), dma((3,)), dma((3,)), dma((9, 2)), dma((9, 2)), dma((9,)), dma((9,)),
-        dma((NS,)), dma((NS,)), dma((NS,)), dma((NS,)), dma((NS,)), dma((NS,)), dma((NS,)), dma((NS,)),
-        dma((NS,)), dma((NS,)),
+        dma((8,)), dma((3,)), dma((3,)), dma((9, 2)), dma((9, 2)), dma((9, 2)), dma((9, 2)),
+        dma((9,)), dma((9,)), dma((3, 2, 4)), dma((3, 2, 4)), dma((2, 4)), dma((2, 4)),
         dma((4,)), dma((4,)),
         dma((6, NC)), dma((6, NC)), dma((6, NC)), dma((6, NC)), dma((6, NC)), dma((6, NC)),
         dma((2,)),

time: 143 us -> 111 us (0.78)
  Pallas kernels: 140 us -> 107 us
    pallas_call x1, Pallas kernels: 140 us -> 107 us  [body(): pl.pallas_call(kernel, out_shape=(jax.ShapeDtypeStruct((ROWS, HD), F32),...]
where the time goes in v2:
time: 111 us
  Pallas kernels  107 us (96%)
  local copies, waits for them, and re-layouts  2.75 us (2%)
    pallas_call x1, Pallas kernels, body(): pl.pallas_call(kernel, out_shape=(jax.ShapeDtypeStruct((ROWS, HD), F32),...  107 us
    unnamed x2, local copies, waits for them, and re-layouts  2.75 us

profile of v2, /device:TPU:1, one launch (start us, length us, event | category | flops | bytes accessed | tf_op | source)
XLA Modules:
  0.0 110.8 jit_solution(4415127161555713378)
XLA Ops:
  0.6 107.5 %shard_map.122 = (f32[64,64]{1,0:T(8,128)}, f32[64,64]{1,0:T(8,128)}) custom-call(s32[8,16]{1,0:T(8,128)} %bitcast.18, f32[64,64]{1,0:T(8,128)} %bitcast.15, f32[8,64]{1,0:T(8,128)} %bitcast.19, bf16[64,3072]{1,0:T(8,128)(2,1)} %patch_h.1, bf16[32,3072]{1,0:T(8,128)(2,1)} %bitcast.14, bf16[6,32,3072]{2,1,0:T(8,128)(2,1)} %bitcast.12, ...), custom_call_target="tpu_custom_call" | custom-call | tf_op jit(solution)/shard_map/pallas_call | solution.py:664
  108.1 1.4 %copy.15 = f32[1,8,8,64]{3,2,1,0:T(8,128)} copy(f32[1,8,8,64]{3,2,1,0:T(8,128)} %bitcast.17) | data formatting | bytes 32768
  109.5 1.4 %copy.16 = f32[1,1,8,8,64]{4,3,2,1,0:T(8,128)} copy(f32[1,1,8,8,64]{4,3,2,1,0:T(8,128)} %bitcast.16) | data formatting | bytes 32768

commit v3 on v2

v3 whole, which is shorter than its diff:
```python
import functools
import math

import jax
import jax.numpy as jnp
from jax import lax
from jax.experimental import pallas as pl
from jax.experimental.pallas import tpu as pltpu
from jax.sharding import PartitionSpec as P

MESH = pl.DeviceIdType.MESH
BF = jnp.bfloat16
F32 = jnp.float32
HD = 64
NT = 1000
NQ = 16
NS = 16
D = 3072
FR = 8
ROWS = 64
TOK = 1024
GROUP = 256
NC = 4
CW = D // NC
NK = 2
CK = D // NK
HR = ROWS // 2
QR = HR // 2
GR = GROUP // 2
FS = 384
HS = 192
M1 = 2 * D // 8
M2 = 4 * D // 8


def noise_level(times):
    angle = (times / NT + 0.008) / 1.008 * (math.pi / 2)
    cosine = jnp.cos(angle)
    return 0.05 + 0.94 * cosine * cosine


def dot_nt(a, b):
    return lax.dot_general(a, b, (((1,), (1,)), ((), ())), preferred_element_type=F32)


def dot(a, b):
    return jnp.dot(a, b, preferred_element_type=F32)


def lnorm(v):
    centre = v - jnp.mean(v, -1, keepdims=True)
    spread = jnp.mean(centre * centre, -1, keepdims=True)
    return centre * lax.rsqrt(spread + 1e-05)


def kernel(
    lev, lat, noise, patch_h, tw_h, ada_h, qkv_h, out_h, up_h, down_h, proj_h,
    both,
    patch, tw, ada, qkv, proj, wo, wu, wd,
    p1, p2, ra1, ra2, rb1, rb2, b1, b2, t1, t2, mod1, mod2,
    xs, xg, xet, acc_m, acc_s, abuf, mt, qt, kn, va, msend, mixt, mixa,
    res, own, s_o, s_r, s_l, p_r, p_l, rl, rr, ol, or_,
    nbuf, hacc, hid, fin, mv, cs, cr,
    lsem, ps, pr, ys, yr, zs, zr, fs, fr, mss, msr, xss, xrs,
    as_, ar, ss, sr, gs, gr, csem,
):
    q = lax.axis_index("queue")
    s = lax.axis_index("space")
    core = lax.rem(s, 2)
    x = lax.rem(s // 2, 4)
    y = s // 8

    def at(y_, x_, c_):
        return (y_ * 4 + x_) * 2 + c_

    mate = at(y, x, 1 - core)
    over = at(1 - y, x, core)
    q_flip = q + 1 - 2 * lax.rem(q, 2)
    right = at(y, lax.rem(x + 1, 4), core)
    left = at(y, lax.rem(x + 3, 4), core)
    q_next = lax.rem(q + 1, NQ)
    q_prev = lax.rem(q + NQ - 1, NQ)

    def local(i, src, dst):
        return pltpu.make_async_copy(src, dst, lsem.at[i])

    def remote(src, dst, ssem, rsem, sp, qq=None):
        return pltpu.make_async_remote_copy(
            src_ref=src, dst_ref=dst, send_sem=ssem, recv_sem=rsem,
            device_id=(q if qq is None else qq, sp), device_id_type=MESH,
        )

    c_tw = local(0, tw_h, tw)
    c_ada = local(1, ada_h, ada)
    c_patch = local(2, patch_h, patch)
    c_qkv = local(3, qkv_h, qkv)
    c_wo = local(4, out_h, wo.at[pl.ds(0, HS)])
    c_wu = local(5, up_h, wu.at[:, pl.ds(0, FS)])
    c_wd = local(6, down_h, wd.at[pl.ds(0, FS)])
    c_proj = local(7, proj_h, proj)
    for c in (c_tw, c_ada, c_patch, c_qkv):
        c.start()

    bar = pltpu.get_barrier_semaphore()

    group = ((mate, 1), (over, 2), (at(1 - y, x, 1 - core), 3))
    ring = ((right, 1), (at(y, lax.rem(x + 2, 4), core), 2), (left, 3))
    par = lax.rem(q // 2, 2)
    z_to = [lax.rem(q + NQ + 2 * (1 - 2 * par) * (1 - 2 * h), NQ) for h in range(2)]
    for dev in (
        [(q, o) for o, _ in group + ring]
        + [(q_flip, over), (q_next, s), (q_prev, s), (z_to[0], s), (z_to[1], s)]
    ):
        pl.semaphore_signal(bar, inc=1, device_id=dev, device_id_type=MESH)

    row = lax.broadcasted_iota(jnp.int32, (FR, 128), 0)
    now = jnp.zeros((FR, 128), F32)
    later = jnp.zeros((FR, 128), F32)
    for f in range(FR):
        t_now = lev[f, q].astype(F32)
        if f < FR - 1:
            t_later = lev[f + 1, q].astype(F32)
        else:
            t_later = lev[0, jnp.minimum(q + 1, NQ - 1)].astype(F32)
        now = jnp.where(row == f, t_now, now)
        later = jnp.where(row == f, t_later, later)
    a_now = noise_level(now)
    a_after = noise_level(later)
    a_after = jnp.where((row == FR - 1) & (q == NQ - 1), 1.0, a_after)
    keep = jnp.sqrt(a_after / a_now)
    mix = jnp.sqrt(1.0 - a_after) - jnp.sqrt(a_after * (1.0 - a_now) / a_now)

    half = D // 2
    lane = lax.broadcasted_iota(jnp.int32, (FR, half), 1).astype(F32)
    freqs = jnp.exp(-math.log(10000.0) * lane / half)
    angle = now[:, 0:1] * freqs
    c_tw.wait()
    pre = dot_nt(jnp.cos(angle).astype(BF), tw[:, 0:half]) + dot_nt(
        jnp.sin(angle).astype(BF), tw[:, half:D]
    )
    timing = (pre * jax.nn.sigmoid(pre)).astype(BF)
    c_ada.wait()
    for k in range(2):
        part = dot(timing, ada[k])
        for h in range(2):
            two = [part[:, (2 * h + i) * M1 : (2 * h + i + 1) * M1] for i in range(2)]
            p1[2 * k + h] = jnp.concatenate(two, 0).astype(BF)

    me4 = y * 2 + core
    pl.semaphore_wait(bar, 11)

    def slot_of(slot):
        return lax.rem(y + slot // 2, 2) * 2 + lax.rem(core + slot, 2)

    def group_sum(k, part, recv):
        ssem, rsem = mss.at[0, k], msr.at[0, k]
        return [
            remote(part.at[slot_of(i)], recv.at[i], ssem.at[i], rsem.at[i], o) for o, i in group
        ]

    def ring_sum(k, mine, recv):
        ssem, rsem = mss.at[1, k], msr.at[1, k]
        return [remote(mine, recv.at[i], ssem.at[i], rsem.at[i], o) for o, i in ring]

    def group_spread(k, tot):
        ssem, rsem = mss.at[2, k], msr.at[2, k]
        return [
            remote(tot.at[me4], tot.at[me4], ssem.at[i], rsem.at[i], o) for o, i in group
        ]

    x_near = [
        remote(xg.at[x, me4], xg.at[x, me4], xss.at[0, i], xrs.at[0, i], o) for o, i in group
    ]
    x_far = [remote(xg.at[x], xg.at[x], xss.at[1, i], xrs.at[1, i], o) for o, i in ring]

    def begin(copies):
        for c in copies:
            c.start()

    def arrive(copies):
        for c in copies:
            c.wait_recv()

    steps = []
    for k, (part, ra, mine, rb, tot) in enumerate(((p1, ra1, b1, rb1, t1), (p2, ra2, b2, rb2, t2))):
        steps.append((group_sum(k, part, ra), ring_sum(k, mine, rb), group_spread(k, tot)))

    def join(k):
        part, ra, mine = ((p1, ra1, b1), (p2, ra2, b2))[k]
        arrive(steps[k][0])
        acc = part[me4].astype(F32)
        for i in range(1, 4):
            acc += ra[i].astype(F32)
        mine[...] = acc.astype(BF)
        begin(steps[k][1])

    def close(k):
        mine, rb, tot = ((b1, rb1, t1), (b2, rb2, t2))[k]
        arrive(steps[k][1])
        acc = mine[...].astype(F32)
        for i in range(1, 4):
            acc += rb[i].astype(F32)
        tot[me4] = acc.astype(BF)
        begin(steps[k][2])

    def unpack(k):
        tot, mod, w = ((t1, mod1, M1), (t2, mod2, M2))[k]
        arrive(steps[k][2])
        for m in range(4):
            v = tot[m].astype(F32)
            mod[:, 2 * m * w : (2 * m + 1) * w] = v[0:FR]
            mod[:, (2 * m + 1) * w : (2 * m + 2) * w] = v[FR : 2 * FR]

    begin(steps[0][0])

    c_patch.wait()
    x_own = lat[...]
    res[...] = dot(x_own.astype(BF), patch[...])
    full = res[...]
    centre = full - jnp.mean(full, -1, keepdims=True)
    spread = jnp.mean(centre * centre, -1, keepdims=True)
    rstd = lax.rsqrt(spread + 1e-05)
    r_hi = rstd.astype(BF).astype(F32)
    r_mid = (rstd - r_hi).astype(BF).astype(F32)
    r_lo = rstd - r_hi - r_mid
    xs[...] = jnp.zeros_like(xs)
    xs[:, 0:HD] = x_own
    lane_x = lax.broadcasted_iota(jnp.int32, (ROWS, 128), 1)
    packed = xs[...]
    packed = jnp.where(lane_x == 64, r_hi, packed)
    packed = jnp.where(lane_x == 65, r_mid, packed)
    packed = jnp.where(lane_x == 66, r_lo, packed)
    xg[x, me4] = packed.astype(BF)
    begin(x_near)

    w_wo = remote(out_h, wo.at[pl.ds(HS, HS)], ps.at[0], pr.at[0], mate)
    w_wu = remote(up_h, wu.at[:, pl.ds(FS, FS)], ps.at[1], pr.at[1], mate)
    w_wd = remote(down_h, wd.at[pl.ds(FS, FS)], ps.at[2], pr.at[2], mate)

    y_pairs = []
    z_sends = []
    z_recvs = []
    f_copies = []

    def piece(i, source, target, forward_from, forward_to):
        mine = [2 * par + h for h in range(2)]
        theirs = [2 * (1 - par) + h for h in range(2)]
        y_pairs.append([
            remote(source(mine[h]), target(mine[h]), ys.at[i, h], yr.at[i, h], over, (q, q_flip)[h])
            for h in range(2)
        ])
        for lst, parts in ((z_sends, mine), (z_recvs, theirs)):
            lst.append([
                remote(target(parts[h]), target(parts[h]), zs.at[i, h], zr.at[i, h], s, z_to[h])
                for h in range(2)
            ])
        f_copies.append(remote(forward_from, forward_to, fs.at[i], fr.at[i], mate))

    def rows_of(base, part, size):
        return pl.ds(pl.multiple_of(base + part * size, 16), size)

    piece(
        0,
        lambda p: out_h.at[rows_of(0, p, HS // 4)],
        lambda p: wo.at[rows_of(2 * HS, p, HS // 4)],
        wo.at[pl.ds(2 * HS, HS)],
        wo.at[pl.ds(3 * HS, HS)],
    )
    for k in range(NC):
        piece(
            1 + k,
            lambda p, k=k: up_h.at[rows_of(k * CW, p, CW // 4)],
            lambda p, k=k: wu.at[rows_of(k * CW, p, CW // 4), pl.ds(2 * FS, FS)],
            wu.at[pl.ds(k * CW, CW), pl.ds(2 * FS, FS)],
            wu.at[pl.ds(k * CW, CW), pl.ds(3 * FS, FS)],
        )
    for k in range(NC):
        piece(
            1 + NC + k,
            lambda p, k=k: down_h.at[rows_of(0, p, FS // 4), pl.ds(k * CW, CW)],
            lambda p, k=k: wd.at[rows_of(2 * FS, p, FS // 4), pl.ds(k * CW, CW)],
            wd.at[pl.ds(2 * FS, FS), pl.ds(k * CW, CW)],
            wd.at[pl.ds(3 * FS, FS), pl.ds(k * CW, CW)],
        )

    def push(i):
        begin(y_pairs[i])

    def along(i):
        arrive(y_pairs[i])
        begin(z_sends[i])

    def forward(i):
        arrive(z_recvs[i])
        f_copies[i].start()

    c_wo.start()
    push(0)
    w_wo.start()
    c_proj.start()

    for k in range(4):
        part = dot(timing, ada[2 + k])
        p2[k] = jnp.concatenate([part[:, 0:M2], part[:, M2 : 2 * M2]], 0).astype(BF)
    join(0)
    arrive(x_near)
    begin(x_far)
    close(0)
    begin(steps[1][0])
    for k in range(NC):
        push(1 + k)
    c_wu.start()
    w_wu.start()

    arrive(x_far)
    halves = [
        xg[b, m, h * HR : (h + 1) * HR] for h in range(2) for m in range(4) for b in range(4)
    ]
    xt = jnp.concatenate(halves, 0).astype(F32).T
    rstd_all = xt[64:65] + xt[65:66] + xt[66:67]
    frame = lax.rem(lax.broadcasted_iota(jnp.int32, (HD, TOK), 1), FR)
    xt = xt[0:HD]
    for f in range(FR):
        xet[f * HD : (f + 1) * HD, :] = jnp.where(frame == f, xt, 0.0).astype(BF)
    hot = (
        lax.rem(lax.broadcasted_iota(jnp.int32, (16, TOK), 1), FR)
        == lax.rem(lax.broadcasted_iota(jnp.int32, (16, TOK), 0), FR)
    ).astype(F32).astype(BF)

    acc_m[...] = jnp.zeros_like(acc_m)
    acc_s[...] = jnp.zeros_like(acc_s)
    hacc[...] = jnp.zeros_like(hacc)
    mean_w = jnp.mean(patch[...].astype(F32), -1, keepdims=True)
    c_qkv.wait()
    unpack(0)
    along(0)

    def fold(j, carry):
        c = pl.ds(pl.multiple_of(j * CW, 128), CW)
        centred = patch[:, c].astype(F32) - mean_w
        gain = 1.0 + mod1[:, pl.ds(pl.multiple_of(D + j * CW, 128), CW)]
        for f in range(FR):
            abuf[f * HD : (f + 1) * HD, :] = (centred * gain[f : f + 1]).astype(BF)
        shift = mod1[:, c]
        hi = shift.astype(BF).astype(F32)
        both = jnp.concatenate([hi, shift - hi], 0).astype(BF)
        w = qkv[:, c]
        acc_m[...] += dot_nt(w, abuf[...])
        acc_s[...] += dot_nt(w, both)
        return carry

    join(1)
    lax.fori_loop(0, NC, fold, 0)
    along(1)
    along(2)
    close(1)
    mt[...] = acc_m[...].astype(BF)
    s_hi = acc_s[...].astype(BF)
    s_lo = (acc_s[...] - s_hi.astype(F32)).astype(BF)

    def project(k):
        r = slice(k * HS, (k + 1) * HS)
        out = dot(mt[r, :], xet[...]) * rstd_all
        return (out + dot(s_hi[r], hot) + dot(s_lo[r], hot)).reshape(3, HD, TOK)

    def head_norm(v):
        centre = v - jnp.mean(v, 1, keepdims=True)
        spread = jnp.mean(centre * centre, 1, keepdims=True)
        return centre * lax.rsqrt(spread + 1e-06)

    queries = head_norm(project(0)) * (HD**-0.5 / math.log(2.0))
    qt[...] = queries.astype(BF)
    keys = head_norm(project(1))
    for h in range(3):
        kn[h] = keys[h].T.astype(BF)
    values = project(2)
    for h in range(3):
        va[h, 0:HD, :] = values[h].astype(BF)
        va[h, HD : HD + 16, :] = jnp.ones((16, TOK), BF)

    def mix_copies(h):
        return [
            remote(msend.at[h, 0, 1 - core], mixt.at[h, 1], as_.at[h, 1], ar.at[h, 1], mate),
            remote(msend.at[h, 1, core], mixt.at[h, 2], as_.at[h, 2], ar.at[h, 2], over),
            remote(msend.at[h, 1, 1 - core], mixt.at[h, 3], as_.at[h, 3], ar.at[h, 3], group[2][0]),
        ]

    def attend(h):
        def part(i, carry):
            flip = 1 - i
            y_ = lax.rem(y + flip, 2)
            g = pl.ds(pl.multiple_of((h * 2 + y_) * GROUP, GROUP), GROUP)
            for n in range(3):
                scores = dot(kn[n], qt[n, :, g])
                weights = jnp.exp2(scores).astype(BF)
                o = dot(va[n], weights)
                o = (o[0:HD] / o[HD : HD + 1]).astype(BF)
                for c in range(2):
                    msend[h, flip, c, n * HD : (n + 1) * HD, :] = o[:, c * GR : (c + 1) * GR]

            @pl.when(i == 0)
            def _():
                begin(mix_copies(h)[1:])

            return carry

        lax.fori_loop(0, 2, part, 0)
        begin(mix_copies(h)[:1])

    def turn(h):
        mixt[h, 0] = msend[h, 0, core]
        arrive(mix_copies(h))
        v = mixt[h].reshape(4 * HS, GR).astype(F32).T.astype(BF)
        for b in range(4):
            o = lax.rem(b - x + 4, 4)
            r = pl.ds(pl.multiple_of(o * HR, HR), HR)
            mixa[h, r, :] = v[b * HR : (b + 1) * HR]

    def chunk(j):
        return pl.ds(pl.multiple_of(j * CK, 128), CK)

    lo, hi16 = pl.ds(0, QR), pl.ds(QR, QR)

    def sends(p, h, j):
        c = chunk(j)

        def to(i, src, rows, dst, dst_rows, dev):
            return remote(
                src.at[h, rows, c], dst.at[p, h, dst_rows, c], ss.at[p, h, j, i], sr.at[p, h, j, i], dev
            )

        return [
            to(0, s_o, lo, ol, lo, right),
            to(1, s_o, hi16, or_, lo, left),
            to(2, s_r, hi16, rl, hi16, right),
            to(3, s_l, lo, rr, lo, left),
            to(4, s_r, lo, rl, lo, right),
            to(5, s_l, hi16, rr, hi16, left),
        ]

    def opened(p, h, term):
        def step(j, carry):
            c = chunk(j)
            v = term(h, c)
            m = sends(p, h, j)
            s_o[h, :, c] = v[2 * HR : 3 * HR].astype(BF)
            begin(m[0:2])
            s_r[h, QR:HR, c] = v[HR + QR : 2 * HR].astype(BF)
            s_l[h, 0:QR, c] = v[3 * HR : 3 * HR + QR].astype(BF)
            begin(m[2:4])
            p_r[h, :, c] = v[HR : HR + QR]
            p_l[h, :, c] = v[3 * HR + QR : 4 * HR]
            own[h, :, c] = v[0:HR]
            return carry

        lax.fori_loop(0, NK, step, 0)

    def passed(p, h):
        def step(j, carry):
            c = chunk(j)
            m = sends(p, h, j)
            m[0].wait_recv()
            s_r[h, 0:QR, c] = (p_r[h, :, c] + ol[p, h, :, c].astype(F32)).astype(BF)
            m[4].start()
            m[1].wait_recv()
            s_l[h, QR:HR, c] = (p_l[h, :, c] + or_[p, h, :, c].astype(F32)).astype(BF)
            m[5].start()
            return carry

        lax.fori_loop(0, NK, step, 0)

    def finish(p, h):
        def step(j, carry):
            arrive(sends(p, h, j)[2:])
            return carry

        lax.fori_loop(0, NK, step, 0)

    def sent(p, h):
        def step(j, carry):
            for c in sends(p, h, j):
                c.wait_send()
            return carry

        lax.fori_loop(0, NK, step, 0)

    def update(i, p, h, gate):
        r = pl.ds(pl.multiple_of(i * 16, 16), 16)
        rows = pl.ds(pl.multiple_of(h * HR + i * 16, 16), 16)
        summed = own[h, r, :] + rl[p, h, r, :].astype(F32) + rr[p, h, r, :].astype(F32)
        gated = mod2[:, gate * D : (gate + 1) * D] * summed.reshape(2, FR, D)
        return r, rows, res[rows, :].reshape(2, FR, D) + gated

    def second(h):
        def step(i, carry):
            r, rows, new = update(i, 0, h, 0)
            res[rows, :] = new.reshape(16, D)
            v = lnorm(new) * (1.0 + mod2[:, 2 * D : 3 * D]) + mod2[:, D : 2 * D]
            nbuf[h, r, :] = v.reshape(16, D).astype(BF)
            return carry

        lax.fori_loop(0, HR // 16, step, 0)

    def last(h):
        def step(i, carry):
            _, rows, new = update(i, 1, h, 3)
            fin[rows, :] = lnorm(new).reshape(16, D).astype(BF)
            return carry

        lax.fori_loop(0, HR // 16, step, 0)

    def gathers(h, j):
        c = chunk(j)

        def go(i, src, dst, dev):
            return remote(
                nbuf.at[h, pl.ds(src, QR), c], nbuf.at[h, pl.ds(dst, QR), c],
                gs.at[h, j, i], gr.at[h, j, i], dev,
            )

        return [
            go(0, 0, 3 * HR, right),
            go(1, QR, HR + QR, left),
            go(2, QR, 3 * HR + QR, right),
            go(3, 0, HR, left),
            go(4, 3 * HR, 2 * HR, right),
            go(5, HR + QR, 2 * HR + QR, left),
        ]

    def gather(h):
        def step(j, carry):
            begin(gathers(h, j)[:4])
            return carry

        lax.fori_loop(0, NK, step, 0)

    def relay(h, j):
        m = gathers(h, j)
        m[0].wait_recv()
        m[4].start()
        m[1].wait_recv()
        m[5].start()

    def widen(h, j):
        arrive(gathers(h, j)[2:])

        def step(n, carry):
            c = pl.ds(pl.multiple_of(n * 512, 512), 512)
            hacc[h, :, c] += dot(nbuf[h, :, j * CK : (j + 1) * CK], wu[j * CK : (j + 1) * CK, c])
            return carry

        lax.fori_loop(0, 3, step, 0)

    def activate(h):
        def step(i, carry):
            r = pl.ds(pl.multiple_of(i * 16, 16), 16)
            hid[h, r, :] = jax.nn.gelu(hacc[h, r, :], approximate=True).astype(BF)
            return carry

        lax.fori_loop(0, GR // 16, step, 0)

    def out_term(h, c):
        return dot(mixa[h], wo[:, c])

    def down_term(h, c):
        return dot(hid[h], wd[:, c])

    attend(0)
    along(3)
    along(4)
    attend(1)
    for k in range(NC):
        push(1 + NC + k)
    forward(0)
    turn(0)
    c_wo.wait()
    w_wo.wait_recv()
    f_copies[0].wait_recv()
    opened(0, 0, out_term)
    turn(1)
    c_wd.start()
    w_wd.start()
    passed(0, 0)
    opened(0, 1, out_term)
    unpack(1)
    forward(1)
    forward(2)
    passed(0, 1)
    along(1 + NC)
    along(2 + NC)
    finish(0, 0)
    second(0)
    gather(0)
    forward(3)
    forward(4)
    finish(0, 1)
    second(1)
    gather(1)
    along(3 + NC)
    along(4 + NC)
    for j in range(NK):
        relay(0, j)
    sent(0, 0)
    sent(0, 1)
    c_wu.wait()
    w_wu.wait_recv()
    for k in range(NC):
        f_copies[1 + k].wait_recv()
    widen(0, 0)
    relay(1, 0)
    widen(0, 1)
    relay(1, 1)
    activate(0)
    for k in range(NC):
        forward(1 + NC + k)
    c_wd.wait()
    w_wd.wait_recv()
    for k in range(NC):
        f_copies[1 + NC + k].wait_recv()
    opened(1, 0, down_term)
    widen(1, 0)
    widen(1, 1)
    activate(1)
    passed(1, 0)
    opened(1, 1, down_term)
    passed(1, 1)
    finish(1, 0)
    last(0)
    finish(1, 1)
    last(1)
    c_proj.wait()
    out = dot_nt(fin[...], proj[...])
    both[0] = out
    moved = keep[:, 0:HD] * lat[...].reshape(FR, FR, HD) + mix[:, 0:HD] * out.reshape(FR, FR, HD)
    mv[...] = jnp.zeros_like(mv)
    mv[:, 0:HD] = moved.reshape(ROWS, HD)
    cs[...] = mv[pl.ds(FR - 1, FR, stride=FR), :]
    carry_copy = remote(cs, cr, csem.at[0], csem.at[1], s, q_next)
    carry_copy.start()
    for f in range(1, FR):
        both[1, pl.ds(f, FR, stride=FR), :] = mv[pl.ds(f - 1, FR, stride=FR), :][:, 0:HD]

    for c in sum((list(t) for p in steps for t in p), x_near + x_far):
        c.wait_send()
    for h in range(2):
        for c in mix_copies(h):
            c.wait_send()
        sent(1, h)
    for c in (w_wo, w_wu, w_wd):
        c.wait_send()
    for pair in y_pairs + z_sends:
        for c in pair:
            c.wait_send()
    for c in f_copies:
        c.wait_send()

    for h in range(2):
        for j in range(NK):
            for c in gathers(h, j):
                c.wait_send()
    carry_copy.wait()
    both[1, pl.ds(0, FR, stride=FR), :] = jnp.where(q == 0, noise[...], cr[:, 0:HD])


def scratch():
    v = pltpu.VMEM
    dma = pltpu.SemaphoreType.DMA
    return [
        v((HD, D), BF), v((32, D), BF), v((6, 32, D), BF), v((3 * HS, D), BF), v((HD, D), BF),
        v((4 * HS, D), BF), v((D, 4 * FS), BF), v((4 * FS, D), BF),
        v((4, 16, M1), BF), v((4, 16, M2), BF), v((4, 16, M1), BF), v((4, 16, M2), BF),
        v((4, 16, M1), BF), v((4, 16, M2), BF), v((16, M1), BF), v((16, M2), BF),
        v((4, 16, M1), BF), v((4, 16, M2), BF), v((FR, 2 * D), F32), v((FR, 4 * D), F32),
        v((ROWS, 128), F32), v((4, 4, ROWS, 128), BF), v((FR * HD, TOK), BF),
        v((3 * HS, FR * HD), F32), v((3 * HS, 16), F32), v((FR * HD, CW), BF),
        v((3 * HS, FR * HD), BF),
        v((3, HD, TOK), BF), v((3, TOK, HD), BF), v((3, HD + 16, TOK), BF),
        v((2, 2, 2, HS, GR), BF), v((2, 4, HS, GR), BF), v((2, GR, 4 * HS), BF),
        v((ROWS, D), F32), v((2, HR, D), F32),
        v((2, HR, D), BF), v((2, HR, D), BF), v((2, HR, D), BF),
        v((2, QR, D), F32), v((2, QR, D), F32),
        v((2, 2, HR, D), BF), v((2, 2, HR, D), BF), v((2, 2, QR, D), BF), v((2, 2, QR, D), BF),
        v((2, GR, D), BF), v((2, GR, 4 * FS), F32), v((2, GR, 4 * FS), BF), v((ROWS, D), BF),
        v((ROWS, 128), F32), v((FR, 128), F32), v((FR, 128), F32),
        dma((8,)), dma((3,)), dma((3,)), dma((9, 2)), dma((9, 2)), dma((9, 2)), dma((9, 2)),
        dma((9,)), dma((9,)), dma((3, 2, 4)), dma((3, 2, 4)), dma((2, 4)), dma((2, 4)),
        dma((2, 4)), dma((2, 4)),
        dma((2, 2, NK, 6)), dma((2, 2, NK, 6)), dma((2, NK, 6)), dma((2, NK, 6)),
        dma((2,)),
    ]


def body(
    latents, fresh_noise, levels, patch_weight, time_weight, adaln_weight, qkv_weight,
    out_weight, up_weight, down_weight, proj_weight,
):
    vm = pl.BlockSpec(memory_space=pltpu.VMEM)
    hbm = pl.BlockSpec(memory_space=pl.ANY)
    both = pl.pallas_call(
        kernel,
        out_shape=jax.ShapeDtypeStruct((2, ROWS, HD), F32),
        in_specs=[pl.BlockSpec(memory_space=pltpu.SMEM), vm, vm] + [hbm] * 8,
        out_specs=vm,
        scratch_shapes=scratch(),
        compiler_params=pltpu.CompilerParams(
            collective_id=0, has_side_effects=True, vmem_limit_bytes=60 * 1024 * 1024
        ),
    )(
        levels.T,
        latents.reshape(ROWS, HD),
        fresh_noise.reshape(FR, HD),
        patch_weight,
        time_weight.T,
        jnp.transpose(adaln_weight, (1, 0, 2)),
        jnp.transpose(qkv_weight, (1, 2, 0)).reshape(3 * HS, D),
        out_weight,
        up_weight,
        down_weight,
        proj_weight.T,
    )
    return both[1].reshape(1, 8, FR, HD), both[0].reshape(1, 1, 8, FR, HD)


def solution(mesh):
    in_specs = (
        P("queue", "space", None, None),
        P(None, "space", None),
        P(),
        P(),
        P(None, "space"),
        P("space", None, None),
        P(None, None, "space"),
        P("space", None),
        P(None, "space"),
        P("space", None),
        P(),
    )
    out_specs = (P("queue", "space", None, None), P(None, "queue", "space", None, None))
    return jax.shard_map(body, mesh=mesh, in_specs=in_specs, out_specs=out_specs, check_vma=False)
```

time: 111 us -> 101 us (0.910); the launches traced: 111 us -> 99.4 us
  Pallas kernels: 107 us -> 97.4 us
  local copies, waits for them, and re-layouts: 2.75 us -> 1.4 us
    pallas_call x1, Pallas kernels: 107 us -> 97.4 us  [body(): pl.pallas_call(kernel, out_shape=jax.ShapeDtypeStruct((2, ROWS, HD), F32)...]
    unnamed x2 -> x0, local copies, waits for them, and re-layouts: 2.75 us -> none
    another operation x0 -> x1, local copies, waits for them, and re-layouts: none -> 1.4 us  [body(): return (both[1].reshape(1, 8, FR, HD), both[0].reshape(1, 1, 8, FR, HD))]
where the time goes in v3:
time: 101 us; the launch traced here: 99.4 us
  Pallas kernels  97.4 us (96%)
  local copies, waits for them, and re-layouts  1.4 us (1%)
    pallas_call x1, Pallas kernels, body(): pl.pallas_call(kernel, out_shape=jax.ShapeDtypeStruct((2, ROWS, HD), F32)...  97.4 us

profile of v3, /device:TPU:1, one launch (start us, length us, event | category | flops | bytes accessed | tf_op | source)
XLA Modules:
  0.0 99.4 jit_solution(5260029698877067922)
XLA Ops:
  0.6 97.4 %shard_map.122 = f32[2,64,64]{2,1,0:T(8,128)} custom-call(s32[8,16]{1,0:T(8,128)} %bitcast.18, f32[64,64]{1,0:T(8,128)} %bitcast.17, f32[8,64]{1,0:T(8,128)} %bitcast.19, bf16[64,3072]{1,0:T(8,128)(2,1)} %patch_h.1, bf16[32,3072]{1,0:T(8,128)(2,1)} %bitcast.16, bf16[6,32,3072]{2,1,0:T(8,128)(2,1)} %bitcast.14, bf16[576,3072]{1,0:T(8,128)(2,1)} %bitcast.13, ...), custom_call_target="tpu_custom_call" | custom-call | tf_op jit(solution)/shard_map/pallas_call | solution.py:699
  98.0 1.4 %slice_bitcast_fusion = (f32[1,1,8,8,64]{4,3,2,1,0:T(8,128)}, f32[1,8,8,64]{3,2,1,0:T(8,128)}) fusion(f32[2,64,64]{2,1,0:T(8,128)} %shard_map.122), kind=kLoop, calls=%fused_computation | loop fusion | bytes 65536 | tf_op jit(solution)/shard_map/reshape;squeeze | solution.py:721

commit v4 on v3

--- a/solution.py
+++ b/solution.py
@@ -299,16 +299,14 @@
     w_wo.start()
     c_proj.start()
 
+    join(0)
+    arrive(x_near)
+    begin(x_far)
     for k in range(4):
         part = dot(timing, ada[2 + k])
         p2[k] = jnp.concatenate([part[:, 0:M2], part[:, M2 : 2 * M2]], 0).astype(BF)
-    join(0)
-    arrive(x_near)
-    begin(x_far)
     close(0)
     begin(steps[1][0])
-    for k in range(NC):
-        push(1 + k)
     c_wu.start()
     w_wu.start()
 
@@ -327,13 +325,15 @@
         == lax.rem(lax.broadcasted_iota(jnp.int32, (16, TOK), 0), FR)
     ).astype(F32).astype(BF)
 
+    along(0)
     acc_m[...] = jnp.zeros_like(acc_m)
     acc_s[...] = jnp.zeros_like(acc_s)
     hacc[...] = jnp.zeros_like(hacc)
     mean_w = jnp.mean(patch[...].astype(F32), -1, keepdims=True)
     c_qkv.wait()
     unpack(0)
-    along(0)
+    push(1)
+    push(2)
 
     def fold(j, carry):
         c = pl.ds(pl.multiple_of(j * CW, 128), CW)
@@ -351,8 +351,6 @@
 
     join(1)
     lax.fori_loop(0, NC, fold, 0)
-    along(1)
-    along(2)
     close(1)
     mt[...] = acc_m[...].astype(BF)
     s_hi = acc_s[...].astype(BF)
@@ -391,9 +389,12 @@
             y_ = lax.rem(y + flip, 2)
             g = pl.ds(pl.multiple_of((h * 2 + y_) * GROUP, GROUP), GROUP)
             for n in range(3):
-                scores = dot(kn[n], qt[n, :, g])
-                weights = jnp.exp2(scores).astype(BF)
-                o = dot(va[n], weights)
+                asked = qt[n, :, g]
+                o = jnp.zeros((HD + 16, GROUP), F32)
+                for k in range(4):
+                    some = slice(k * GROUP, (k + 1) * GROUP)
+                    weights = jnp.exp2(dot(kn[n, some, :], asked)).astype(BF)
+                    o += dot(va[n, :, some], weights)
                 o = (o[0:HD] / o[HD : HD + 1]).astype(BF)
                 for c in range(2):
                     msend[h, flip, c, n * HD : (n + 1) * HD, :] = o[:, c * GR : (c + 1) * GR]
@@ -438,8 +439,12 @@
             to(5, s_l, hi16, rr, hi16, left),
         ]
 
-    def opened(p, h, term):
+    def opened(p, h, term, late=()):
         def step(j, carry):
+            @pl.when(j > 0)
+            def _():
+                arrive(late)
+
             c = chunk(j)
             v = term(h, c)
             m = sends(p, h, j)
@@ -565,19 +570,21 @@
     def down_term(h, c):
         return dot(hid[h], wd[:, c])
 
+    forward(0)
     attend(0)
-    along(3)
-    along(4)
+    along(1)
+    along(2)
     attend(1)
-    for k in range(NC):
-        push(1 + NC + k)
-    forward(0)
     turn(0)
+    push(3)
+    push(4)
     c_wo.wait()
     w_wo.wait_recv()
     f_copies[0].wait_recv()
     opened(0, 0, out_term)
     turn(1)
+    for k in range(NC):
+        push(1 + NC + k)
     c_wd.start()
     w_wd.start()
     passed(0, 0)
@@ -586,18 +593,18 @@
     forward(1)
     forward(2)
     passed(0, 1)
-    along(1 + NC)
-    along(2 + NC)
+    along(3)
+    along(4)
     finish(0, 0)
     second(0)
     gather(0)
-    forward(3)
-    forward(4)
     finish(0, 1)
     second(1)
     gather(1)
-    along(3 + NC)
-    along(4 + NC)
+    forward(3)
+    forward(4)
+    along(1 + NC)
+    along(2 + NC)
     for j in range(NK):
         relay(0, j)
     sent(0, 0)
@@ -606,18 +613,21 @@
     w_wu.wait_recv()
     for k in range(NC):
         f_copies[1 + k].wait_recv()
+    along(3 + NC)
+    along(4 + NC)
     widen(0, 0)
     relay(1, 0)
+    forward(1 + NC)
+    forward(2 + NC)
     widen(0, 1)
     relay(1, 1)
     activate(0)
-    for k in range(NC):
-        forward(1 + NC + k)
+    forward(3 + NC)
+    forward(4 + NC)
     c_wd.wait()
     w_wd.wait_recv()
-    for k in range(NC):
-        f_copies[1 + NC + k].wait_recv()
-    opened(1, 0, down_term)
+    arrive(f_copies[1 + NC : 3 + NC])
+    opened(1, 0, down_term, f_copies[3 + NC :])
     widen(1, 0)
     widen(1, 1)
     activate(1)

time: 101 us -> 95.5 us (0.946); the launches traced: 99.4 us -> 95.2 us
  Pallas kernels: 97.4 us -> 93.2 us
    pallas_call x1, Pallas kernels: 97.4 us -> 93.2 us  [body(): pl.pallas_call(kernel, out_shape=jax.ShapeDtypeStruct((2, ROWS, HD), F32)...]
where the time goes in v4:
time: 95.5 us; the launch traced here: 95.2 us
  Pallas kernels  93.2 us (98%)
  local copies, waits for them, and re-layouts  1.4 us (1%)
    pallas_call x1, Pallas kernels, body(): pl.pallas_call(kernel, out_shape=jax.ShapeDtypeStruct((2, ROWS, HD), F32)...  93.2 us

profile of v4, /device:TPU:1, one launch (start us, length us, event | category | flops | bytes accessed | tf_op | source)
XLA Modules:
  0.0 95.2 jit_solution(10140210759569002357)
XLA Ops:
  0.6 93.2 %shard_map.122 = f32[2,64,64]{2,1,0:T(8,128)} custom-call(s32[8,16]{1,0:T(8,128)} %bitcast.18, f32[64,64]{1,0:T(8,128)} %bitcast.17, f32[8,64]{1,0:T(8,128)} %bitcast.19, bf16[64,3072]{1,0:T(8,128)(2,1)} %patch_h.1, bf16[32,3072]{1,0:T(8,128)(2,1)} %bitcast.16, bf16[6,32,3072]{2,1,0:T(8,128)(2,1)} %bitcast.14, bf16[576,3072]{1,0:T(8,128)(2,1)} %bitcast.13, ...), custom_call_target="tpu_custom_call" | custom-call | tf_op jit(solution)/shard_map/pallas_call | solution.py:709
  93.8 1.4 %slice_bitcast_fusion = (f32[1,1,8,8,64]{4,3,2,1,0:T(8,128)}, f32[1,8,8,64]{3,2,1,0:T(8,128)}) fusion(f32[2,64,64]{2,1,0:T(8,128)} %shard_map.122), kind=kLoop, calls=%fused_computation | loop fusion | bytes 65536 | tf_op jit(solution)/shard_map/reshape;squeeze | solution.py:731

commit v5 on v4

--- a/solution.py
+++ b/solution.py
@@ -321,8 +321,8 @@
     for f in range(FR):
         xet[f * HD : (f + 1) * HD, :] = jnp.where(frame == f, xt, 0.0).astype(BF)
     hot = (
-        lax.rem(lax.broadcasted_iota(jnp.int32, (16, TOK), 1), FR)
-        == lax.rem(lax.broadcasted_iota(jnp.int32, (16, TOK), 0), FR)
+        lax.rem(lax.broadcasted_iota(jnp.int32, (32, TOK), 1), FR)
+        == lax.rem(lax.broadcasted_iota(jnp.int32, (32, TOK), 0), FR)
     ).astype(F32).astype(BF)
 
     along(0)
@@ -335,31 +335,36 @@
     push(1)
     push(2)
 
-    def fold(j, carry):
+    def fold_one(j, b):
         c = pl.ds(pl.multiple_of(j * CW, 128), CW)
         centred = patch[:, c].astype(F32) - mean_w
         gain = 1.0 + mod1[:, pl.ds(pl.multiple_of(D + j * CW, 128), CW)]
         for f in range(FR):
-            abuf[f * HD : (f + 1) * HD, :] = (centred * gain[f : f + 1]).astype(BF)
+            abuf[b, f * HD : (f + 1) * HD, :] = (centred * gain[f : f + 1]).astype(BF)
         shift = mod1[:, c]
         hi = shift.astype(BF).astype(F32)
         both = jnp.concatenate([hi, shift - hi], 0).astype(BF)
         w = qkv[:, c]
-        acc_m[...] += dot_nt(w, abuf[...])
+        acc_m[...] += dot_nt(w, abuf[b])
         acc_s[...] += dot_nt(w, both)
+
+    def fold(i, carry):
+        fold_one(2 * i, 0)
+        fold_one(2 * i + 1, 1)
         return carry
 
     join(1)
-    lax.fori_loop(0, NC, fold, 0)
+    lax.fori_loop(0, NC // 2, fold, 0)
     close(1)
     mt[...] = acc_m[...].astype(BF)
     s_hi = acc_s[...].astype(BF)
     s_lo = (acc_s[...] - s_hi.astype(F32)).astype(BF)
+    s_all = jnp.concatenate([s_hi, s_lo], 1)
 
     def project(k):
         r = slice(k * HS, (k + 1) * HS)
         out = dot(mt[r, :], xet[...]) * rstd_all
-        return (out + dot(s_hi[r], hot) + dot(s_lo[r], hot)).reshape(3, HD, TOK)
+        return (out + dot(s_all[r], hot)).reshape(3, HD, TOK)
 
     def head_norm(v):
         centre = v - jnp.mean(v, 1, keepdims=True)
@@ -575,9 +580,9 @@
     along(1)
     along(2)
     attend(1)
-    turn(0)
     push(3)
     push(4)
+    turn(0)
     c_wo.wait()
     w_wo.wait_recv()
     f_copies[0].wait_recv()
@@ -592,9 +597,9 @@
     unpack(1)
     forward(1)
     forward(2)
-    passed(0, 1)
     along(3)
     along(4)
+    passed(0, 1)
     finish(0, 0)
     second(0)
     gather(0)
@@ -611,14 +616,14 @@
     sent(0, 1)
     c_wu.wait()
     w_wu.wait_recv()
-    for k in range(NC):
-        f_copies[1 + k].wait_recv()
+    arrive(f_copies[1:3])
     along(3 + NC)
     along(4 + NC)
     widen(0, 0)
     relay(1, 0)
     forward(1 + NC)
     forward(2 + NC)
+    arrive(f_copies[3:5])
     widen(0, 1)
     relay(1, 1)
     activate(0)
@@ -682,7 +687,7 @@
         v((4, 16, M1), BF), v((4, 16, M2), BF), v((16, M1), BF), v((16, M2), BF),
         v((4, 16, M1), BF), v((4, 16, M2), BF), v((FR, 2 * D), F32), v((FR, 4 * D), F32),
         v((ROWS, 128), F32), v((4, 4, ROWS, 128), BF), v((FR * HD, TOK), BF),
-        v((3 * HS, FR * HD), F32), v((3 * HS, 16), F32), v((FR * HD, CW), BF),
+        v((3 * HS, FR * HD), F32), v((3 * HS, 16), F32), v((2, FR * HD, CW), BF),
         v((3 * HS, FR * HD), BF),
         v((3, HD, TOK), BF), v((3, TOK, HD), BF), v((3, HD + 16, TOK), BF),
         v((2, 2, 2, HS, GR), BF), v((2, 4, HS, GR), BF), v((2, GR, 4 * HS), BF),

time: 95.5 us -> 92 us (0.963)
  Pallas kernels: 93.2 us -> 89.7 us
    pallas_call x1, Pallas kernels: 93.2 us -> 89.7 us  [body(): pl.pallas_call(kernel, out_shape=jax.ShapeDtypeStruct((2, ROWS, HD), F32)...]
where the time goes in v5:
time: 92 us; the launch traced here: 91.7 us
  Pallas kernels  89.7 us (98%)
  local copies, waits for them, and re-layouts  1.4 us (2%)
    pallas_call x1, Pallas kernels, body(): pl.pallas_call(kernel, out_shape=jax.ShapeDtypeStruct((2, ROWS, HD), F32)...  89.7 us

profile of v5, /device:TPU:1, one launch (start us, length us, event | category | flops | bytes accessed | tf_op | source)
XLA Modules:
  0.0 91.7 jit_solution(11693177823437452536)
XLA Ops:
  0.6 89.7 %shard_map.122 = f32[2,64,64]{2,1,0:T(8,128)} custom-call(s32[8,16]{1,0:T(8,128)} %bitcast.18, f32[64,64]{1,0:T(8,128)} %bitcast.17, f32[8,64]{1,0:T(8,128)} %bitcast.19, bf16[64,3072]{1,0:T(8,128)(2,1)} %patch_h.1, bf16[32,3072]{1,0:T(8,128)(2,1)} %bitcast.16, bf16[6,32,3072]{2,1,0:T(8,128)(2,1)} %bitcast.14, bf16[576,3072]{1,0:T(8,128)(2,1)} %bitcast.13, ...), custom_call_target="tpu_custom_call" | custom-call | tf_op jit(solution)/shard_map/pallas_call | solution.py:714
  90.3 1.4 %slice_bitcast_fusion = (f32[1,1,8,8,64]{4,3,2,1,0:T(8,128)}, f32[1,8,8,64]{3,2,1,0:T(8,128)}) fusion(f32[2,64,64]{2,1,0:T(8,128)} %shard_map.122), kind=kLoop, calls=%fused_computation | loop fusion | bytes 65536 | tf_op jit(solution)/shard_map/reshape;squeeze | solution.py:736

commit v6 on v5

--- a/solution.py
+++ b/solution.py
@@ -603,13 +603,13 @@
     finish(0, 0)
     second(0)
     gather(0)
+    along(1 + NC)
+    along(2 + NC)
     finish(0, 1)
     second(1)
     gather(1)
     forward(3)
     forward(4)
-    along(1 + NC)
-    along(2 + NC)
     for j in range(NK):
         relay(0, j)
     sent(0, 0)

time: 92 us -> 90.9 us (0.988)
  Pallas kernels: 89.7 us -> 88.2 us
    pallas_call x1, Pallas kernels: 89.7 us -> 88.2 us  [body(): pl.pallas_call(kernel, out_shape=jax.ShapeDtypeStruct((2, ROWS, HD), F32)...]
where the time goes in v6:
time: 90.9 us; the launch traced here: 90.2 us
  Pallas kernels  88.2 us (97%)
  local copies, waits for them, and re-layouts  1.4 us (2%)
    pallas_call x1, Pallas kernels, body(): pl.pallas_call(kernel, out_shape=jax.ShapeDtypeStruct((2, ROWS, HD), F32)...  88.2 us

profile of v6, /device:TPU:1, one launch (start us, length us, event | category | flops | bytes accessed | tf_op | source)
XLA Modules:
  0.0 90.2 jit_solution(14763198182125092158)
XLA Ops:
  0.6 88.2 %shard_map.122 = f32[2,64,64]{2,1,0:T(8,128)} custom-call(s32[8,16]{1,0:T(8,128)} %bitcast.18, f32[64,64]{1,0:T(8,128)} %bitcast.17, f32[8,64]{1,0:T(8,128)} %bitcast.19, bf16[64,3072]{1,0:T(8,128)(2,1)} %patch_h.1, bf16[32,3072]{1,0:T(8,128)(2,1)} %bitcast.16, bf16[6,32,3072]{2,1,0:T(8,128)(2,1)} %bitcast.14, bf16[576,3072]{1,0:T(8,128)(2,1)} %bitcast.13, ...), custom_call_target="tpu_custom_call" | custom-call | tf_op jit(solution)/shard_map/pallas_call | solution.py:714
  88.8 1.4 %slice_bitcast_fusion = (f32[1,1,8,8,64]{4,3,2,1,0:T(8,128)}, f32[1,8,8,64]{3,2,1,0:T(8,128)}) fusion(f32[2,64,64]{2,1,0:T(8,128)} %shard_map.122), kind=kLoop, calls=%fused_computation | loop fusion | bytes 65536 | tf_op jit(solution)/shard_map/reshape;squeeze | solution.py:736
